TPU v7x, 32 devices: a whole 2x2x4 slice. The times are simulated.
32 devices in a mesh: groups: 2 (over x), gx: 16 (over z, y, core).
Axes of the slice: x: 2, y: 2, z: 4, core: 2. Of those that a mesh axis runs over, the one named last changes fastest.
Arguments:
- velocity: float32 [3, 32, 4, 32, 128], P(None, ('groups', 'gx')), parts along dimension 1, may hold values from -6 to 6
- stress: float32 [6, 32, 4, 32, 128], P(None, ('groups', 'gx')), parts along dimension 1, may hold values from -6 to 6
- memory: float32 [6, 32, 4, 32, 128], P(None, ('groups', 'gx')), parts along dimension 1, may hold values from -4 to 4
- lame_lambda: float32 [32, 4, 32, 128], P(('groups', 'gx')), parts along dimension 0, may hold values from 1.5 to 2.5
- lame_mu: float32 [32, 4, 32, 128], P(('groups', 'gx')), parts along dimension 0, may hold values from 0.1 to 0.5
- buoyancy: float32 [32, 4, 32, 128], P(('groups', 'gx')), parts along dimension 0, may hold values from 0.7 to 1
- decay: float32 [32, 4, 32, 128], P(('groups', 'gx')), parts along dimension 0, may hold values from 0.3 to 0.95
- loss: float32 [32, 4, 32, 128], P(('groups', 'gx')), parts along dimension 0, may hold values from 0.1 to 1
- tile_lambda: bfloat16 [256, 256], P(('groups', 'gx')), parts along dimension 0, may hold values from 3 to 4.5
- tile_mu: bfloat16 [256, 256], P(('groups', 'gx')), parts along dimension 0, may hold values from 1 to 2
- tile_buoy: bfloat16 [256, 256], P(('groups', 'gx')), parts along dimension 0, may hold values from 0.3984375 to 0.59765625
- tile_dest: int32 [256], P(('groups', 'gx')), parts along dimension 0, may hold values from -1 to 15, as said below
- brick_tiles: int32 [32, 64], P(('groups', 'gx')), parts along dimension 0, may hold values from -1 to 127, as said below
- src_index: int32 [512], P(('groups', 'gx')), parts along dimension 0, may hold values from 0 to 16383
- src_wave: float32 [512, 2], P(('groups', 'gx')), parts along dimension 0, may hold values from -6 to 6
Outputs:
- new_velocity: float32 [3, 32, 4, 32, 128], P(None, ('groups', 'gx')), parts along dimension 1
- new_stress: float32 [6, 32, 4, 32, 128], P(None, ('groups', 'gx')), parts along dimension 1
- new_memory: float32 [6, 32, 4, 32, 128], P(None, ('groups', 'gx')), parts along dimension 1
There are 2 independent parts, one for each index of `groups`. A program takes and returns all parts, laid end to end along the dimension named above; each array names one. Nothing has to cross between parts.
Inputs may be any that keep to these rules, and one draw needn't show every extreme that they name: `tile_dest`: the 8 tiles stored on one device name distinct bricks; a brick receives at most 8 tiles, and some brick exactly 8 in every draw. `brick_tiles`: row b holds, at distinct positions, exactly the tiles whose tile_dest is b, each once.
All inputs are finite; a program needn't handle non-finite values.
Results may differ from a plain program's by a relative error of at most 0.00075.
Values may be sent and summed in bfloat16 or wider, within the bound.
A program may use at most 64 MiB of HBM per device.

v0:
```python
import jax
import jax.numpy as jnp
from jax import lax
from jax.sharding import PartitionSpec as P

PY = 8
TY = 8
TZ = 8


courant = 0.25


def passed_along(block, axis, distance):
    devices = range(lax.axis_size(axis))
    route = [(i - distance, i) for i in devices if i - distance in devices]
    return lax.ppermute(block, axis, route)


def shifted(array, axis, by):
    count = lax.axis_size(axis)
    return lax.ppermute(array, axis, [(i, (i + by) % count) for i in range(count)])


def forward_diff(values, along):
    rest = lax.slice_in_dim(values, 1, values.shape[along], axis=along)
    padding = jnp.zeros_like(lax.slice_in_dim(values, 0, 1, axis=along))
    return jnp.concatenate([rest, padding], axis=along) - values


def backward_diff(values, along):
    padding = jnp.zeros_like(lax.slice_in_dim(values, 0, 1, axis=along))
    rest = lax.slice_in_dim(values, 0, values.shape[along] - 1, axis=along)
    return values - jnp.concatenate([padding, rest], axis=along)


def forward_with(values, after, along):
    rest = lax.slice_in_dim(values, 1, values.shape[along], axis=along)
    return jnp.concatenate([rest, after], axis=along) - values


def backward_with(values, before, along):
    rest = lax.slice_in_dim(values, 0, values.shape[along] - 1, axis=along)
    return values - jnp.concatenate([before, rest], axis=along)


def neighbours(ahead_x, behind_x, ahead_y, behind_y):
    got_ahead_x = passed_along(ahead_x.astype(jnp.bfloat16), "gx", -PY).astype(ahead_x.dtype)
    got_behind_x = passed_along(behind_x, "gx", PY)
    got_ahead_y = shifted(ahead_y, "gx", -1)
    got_behind_y = shifted(behind_y, "gx", 1)
    return (got_ahead_x, got_behind_x, got_ahead_y, got_behind_y)


def stress_faces(stress):
    return neighbours(stress[0:1, :1], stress[3:5, -1:], stress[1:2, :, :1], stress[3::2, :, -1:])


def velocity_faces(velocity):
    return neighbours(
        velocity[1:3, :1], velocity[0:1, -1:], velocity[0::2, :, :1], velocity[1:2, :, -1:]
    )


def body(
    velocity,
    stress,
    memory,
    lame_lambda,
    lame_mu,
    buoyancy,
    decay,
    loss,
    tile_lambda,
    tile_mu,
    tile_buoy,
    tile_dest,
    brick_tiles,
    src_index,
    src_wave,
):
    bricks = lax.axis_size("gx")
    per_device = tile_lambda.shape[0]
    width_x, width_y, width_z = lame_lambda.shape[1:]
    rows_y = width_y // TY
    rows_z = width_z // TZ
    brick_ids = jnp.arange(bricks, dtype=jnp.int32)
    route = (tile_dest[None, :] == brick_ids[:, None]).astype(jnp.bfloat16)

    def pack(tiles):
        return jnp.dot(route, tiles, preferred_element_type=jnp.float32).astype(jnp.bfloat16)

    arrived = (
        lax.all_to_all(pack(tile_lambda), "gx", split_axis=0, concat_axis=0, tiled=True),
        lax.all_to_all(pack(tile_mu), "gx", split_axis=0, concat_axis=0, tiled=True),
        lax.all_to_all(pack(tile_buoy), "gx", split_axis=0, concat_axis=0, tiled=True),
    )
    wanted = brick_tiles[0]
    owner = jnp.where(wanted >= 0, wanted // per_device, -1)
    select = (owner[:, None] == brick_ids[None, :]).astype(jnp.bfloat16)
    live = (wanted >= 0).reshape(rows_y, rows_z)
    inside = jnp.broadcast_to(
        live[None, :, None, :, None], (width_x, rows_y, TY, rows_z, TZ)
    ).reshape(width_x, width_y, width_z)

    def place(background, received):
        picked = jnp.dot(select, received, preferred_element_type=jnp.float32)
        picked = (
            picked.reshape(rows_y, rows_z, width_x, TY, TZ)
            .transpose(2, 0, 3, 1, 4)
            .reshape(width_x, width_y, width_z)
        )
        return jnp.where(inside, picked, background)

    lame = place(lame_lambda[0], arrived[0])
    shear = place(lame_mu[0], arrived[1])
    buoy_field = place(buoyancy[0], arrived[2])
    decay_here = decay[0]
    loss_here = loss[0]
    fields_v = velocity[:, 0]
    fields_s = stress[:, 0]
    fields_m = memory[:, 0]
    for step_index in range(src_wave.shape[1]):
        ahead_xs, behind_xs, ahead_ys, behind_ys = stress_faces(fields_s)
        grad_x = (
            forward_with(fields_s[0], ahead_xs[0], 0)
            + backward_with(fields_s[3], behind_ys[0], 1)
            + backward_diff(fields_s[4], 2)
        )
        grad_y = (
            backward_with(fields_s[3], behind_xs[0], 0)
            + forward_with(fields_s[1], ahead_ys[0], 1)
            + backward_diff(fields_s[5], 2)
        )
        grad_z = (
            backward_with(fields_s[4], behind_xs[1], 0)
            + backward_with(fields_s[5], behind_ys[1], 1)
            + forward_diff(fields_s[2], 2)
        )
        fields_v = fields_v + courant * buoy_field * jnp.stack([grad_x, grad_y, grad_z])
        ahead_xv, behind_xv, ahead_yv, behind_yv = velocity_faces(fields_v)
        strain_x = backward_with(fields_v[0], behind_xv[0], 0)
        strain_y = backward_with(fields_v[1], behind_yv[0], 1)
        strain_z = backward_diff(fields_v[2], 2)
        dilation = strain_x + strain_y + strain_z
        rates = jnp.stack(
            [
                lame * dilation + 2.0 * shear * strain_x,
                lame * dilation + 2.0 * shear * strain_y,
                lame * dilation + 2.0 * shear * strain_z,
                shear
                * (
                    forward_with(fields_v[0], ahead_yv[0], 1)
                    + forward_with(fields_v[1], ahead_xv[0], 0)
                ),
                shear * (forward_diff(fields_v[0], 2) + forward_with(fields_v[2], ahead_xv[1], 0)),
                shear * (forward_diff(fields_v[1], 2) + forward_with(fields_v[2], ahead_yv[1], 1)),
            ]
        )
        fields_m = decay_here * fields_m - (1.0 - decay_here) * loss_here * rates
        fields_s = fields_s + courant * (rates + fields_m)
        source = (
            jnp.zeros((width_x * width_y * width_z,), jnp.float32)
            .at[src_index]
            .add(src_wave[:, step_index])
            .reshape(width_x, width_y, width_z)
        )
        fields_s = fields_s.at[:3].add(source[None])
    return (fields_v[:, None], fields_s[:, None], fields_m[:, None])


def solution(mesh):
    return jax.shard_map(
        body,
        mesh=mesh,
        in_specs=(
            P(None, ("groups", "gx"), None, None, None),
            P(None, ("groups", "gx"), None, None, None),
            P(None, ("groups", "gx"), None, None, None),
            P(("groups", "gx"), None, None, None),
            P(("groups", "gx"), None, None, None),
            P(("groups", "gx"), None, None, None),
            P(("groups", "gx"), None, None, None),
            P(("groups", "gx"), None, None, None),
            P(("groups", "gx"), None),
            P(("groups", "gx"), None),
            P(("groups", "gx"), None),
            P(("groups", "gx")),
            P(("groups", "gx"), None),
            P(("groups", "gx")),
            P(("groups", "gx"), None),
        ),
        out_specs=(
            P(None, ("groups", "gx"), None, None, None),
            P(None, ("groups", "gx"), None, None, None),
            P(None, ("groups", "gx"), None, None, None),
        ),
        check_vma=False,
    )
```

profile of v0, /device:TPU:0, one launch (start us, length us, event | category | flops | bytes accessed | tf_op | source)
XLA Modules:
  0.0 102.7 jit_solution(5612992693066059963)
XLA Ops:
  0.7 0.8 slice.652
  1.4 1.3 %collective-permute-start = (bf16[1,1,32,128]{3,2,1,0:T(8,128)(2,1)S(1)}, bf16[1,1,32,128]{3,2,1,0:T(8,128)(2,1)S(1)}, u32[]{:S(2)}, u32[]{:S(2)}) collective-permute-start(bf16[1,1,32,128]{3,2,1,0:T(8,128)(2,1)S(1)} %slice.652), channel_id=1, source_target_pairs={{8,0},{9,1},{10,2},{11,3},{12,4},{13,5},{14,6},{15,7},{24,16},{25,... | collective-permute-start | bytes 24584 | tf_op jit(solution)/shard_map/ppermute | solution.py:17
  2.7 0.8 slice.405
  4.0 1.4 %slice.504 = f32[2,1,32,128]{3,2,1,0:T(8,128)} slice(f32[6,4,32,128]{3,2,1,0:T(8,128)} %bitcast.340), slice={[3:5], [3:4], [0:32], [0:128]} | slice | bytes 65536 | tf_op jit(solution)/shard_map/slice | solution.py:56
  5.3 6.1 %collective-permute-start.2 = (f32[2,1,32,128]{3,2,1,0:T(8,128)}, f32[2,1,32,128]{3,2,1,0:T(8,128)}, u32[]{:S(2)}, u32[]{:S(2)}) collective-permute-start(f32[2,1,32,128]{3,2,1,0:T(8,128)} %slice.504), channel_id=1, source_target_pairs={{0,8},{1,9},{2,10},{3,11},{4,12},{5,13},{6,14},{7,15},{16,24},{17,... | collective-permute-start | bytes 98312 | tf_op jit(solution)/shard_map/ppermute | solution.py:17
  11.4 1.3 %slice.507 = f32[1,4,1,128]{3,2,1,0:T(1,128)} slice(f32[6,4,32,128]{3,2,1,0:T(8,128)} %bitcast.341), slice={[1:2], [0:4], [0:1], [0:128]} | slice | bytes 4096 | tf_op jit(solution)/shard_map/slice | solution.py:56
  12.7 0.9 collective-permute-start.3
  13.6 0.8 fusion.2
  16.1 5.5 %all-to-all-start.2 = ((bf16[16,2,128]{2,1,0:T(2,128)(2,1)}), bf16[16,2,128]{2,1,0:T(2,128)(2,1)S(1)}, u32[]{:S(2)}, u32[]{:S(2)}) async-start(bf16[16,2,128]{2,1,0:T(2,128)(2,1)} %reshape.547), calls=%async_computation.2 | async-start | bytes 16384 | tf_op jit(solution)/shard_map/all_to_all | solution.py:95
  21.5 0.9 fusion.54
  25.9 0.7 copy_bitcast_fusion.5
  28.3 0.7 slice.512
  36.4 6.0 %all-to-all-start = ((bf16[16,2,128]{2,1,0:T(2,128)(2,1)}), bf16[16,2,128]{2,1,0:T(2,128)(2,1)S(1)}, u32[]{:S(2)}, u32[]{:S(2)}) async-start(bf16[16,2,128]{2,1,0:T(2,128)(2,1)} %reshape.543), calls=%async_computation | async-start | bytes 16384 | tf_op jit(solution)/shard_map/all_to_all | solution.py:96
  43.1 5.6 %all-to-all-done = bf16[16,2,128]{2,1,0:T(2,128)(2,1)S(1)} async-done(((bf16[16,2,128]{2,1,0:T(2,128)(2,1)}), bf16[16,2,128]{2,1,0:T(2,128)(2,1)S(1)}, u32[]{:S(2)}, u32[]{:S(2)}) %all-to-all-start) | async-done | bytes 8224 | tf_op jit(solution)/shard_map/all_to_all | solution.py:96
  48.8 3.4 %all-to-all-start.1 = ((bf16[16,2,128]{2,1,0:T(2,128)(2,1)}), bf16[16,2,128]{2,1,0:T(2,128)(2,1)S(1)}, u32[]{:S(2)}, u32[]{:S(2)}) async-start(bf16[16,2,128]{2,1,0:T(2,128)(2,1)} %reshape.545), calls=%async_computation.1 | async-start | bytes 16384 | tf_op jit(solution)/shard_map/all_to_all | solution.py:94
  54.7 3.8 %all-to-all-done.1 = bf16[16,2,128]{2,1,0:T(2,128)(2,1)S(1)} async-done(((bf16[16,2,128]{2,1,0:T(2,128)(2,1)}), bf16[16,2,128]{2,1,0:T(2,128)(2,1)S(1)}, u32[]{:S(2)}, u32[]{:S(2)}) %all-to-all-start.1) | async-done | bytes 8224 | tf_op jit(solution)/shard_map/all_to_all | solution.py:94
  62.5 0.8 fusion.57
  63.3 0.9 fusion.16
  66.8 1.3 %collective-permute-start.7 = (bf16[2,1,32,128]{3,2,1,0:T(8,128)(2,1)S(1)}, bf16[2,1,32,128]{3,2,1,0:T(8,128)(2,1)S(1)}, u32[]{:S(2)}, u32[]{:S(2)}) collective-permute-start(bf16[2,1,32,128]{3,2,1,0:T(8,128)(2,1)S(1)} %copy.373), channel_id=1, source_target_pairs={{8,0},{9,1},{10,2},{11,3},{12,4},{13,5},{14,6},{15,7},{24,16},{25,... | collective-permute-start | bytes 49160 | tf_op jit(solution)/shard_map/ppermute | solution.py:17
  68.2 5.4 %collective-permute-start.4 = (f32[1,1,32,128]{3,1,2,0:T(1,128)S(1)}, f32[1,1,32,128]{3,1,2,0:T(1,128)S(1)}, u32[]{:S(2)}, u32[]{:S(2)}) collective-permute-start(f32[1,1,32,128]{3,1,2,0:T(1,128)S(1)} %slice.514), channel_id=1, source_target_pairs={{0,8},{1,9},{2,10},{3,11},{4,12},{5,13},{6,14},{7,15},{16,24},{17,... | collective-permute-start | bytes 49160 | tf_op jit(solution)/shard_map/ppermute | solution.py:17
  74.1 1.0 collective-permute-done.4
  75.5 0.9 copy-done.1
  76.5 0.8 copy-done.7
  77.7 1.3 %collective-permute-start.8 = (bf16[1,1,32,128]{3,2,1,0:T(8,128)(2,1)S(1)}, bf16[1,1,32,128]{3,2,1,0:T(8,128)(2,1)S(1)}, u32[]{:S(2)}, u32[]{:S(2)}) collective-permute-start(bf16[1,1,32,128]{3,2,1,0:T(8,128)(2,1)S(1)} %copy.396), channel_id=1, source_target_pairs={{8,0},{9,1},{10,2},{11,3},{12,4},{13,5},{14,6},{15,7},{24,16},{25,... | collective-permute-start | bytes 24584 | tf_op jit(solution)/shard_map/ppermute | solution.py:17
  79.5 5.2 %collective-permute-start.10 = (f32[2,1,32,128]{3,2,1,0:T(8,128)S(1)}, f32[2,1,32,128]{3,2,1,0:T(8,128)S(1)}, u32[]{:S(2)}, u32[]{:S(2)}) collective-permute-start(f32[2,1,32,128]{3,2,1,0:T(8,128)S(1)} %slice.541), channel_id=1, source_target_pairs={{0,8},{1,9},{2,10},{3,11},{4,12},{5,13},{6,14},{7,15},{16,24},{17,... | collective-permute-start | bytes 98312 | tf_op jit(solution)/shard_map/ppermute | solution.py:17
  85.3 1.0 collective-permute-done.10
  87.2 4.5 %collective-permute-start.14 = (f32[2,4,1,128]{3,1,2,0:T(4,128)S(1)}, f32[2,4,1,128]{3,1,2,0:T(4,128)S(1)}, u32[]{:S(2)}, u32[]{:S(2)}) collective-permute-start(f32[2,4,1,128]{3,1,2,0:T(4,128)S(1)} %slice.486), channel_id=1, source_target_pairs={{0,15},{1,0},{2,1},{3,2},{4,3},{5,4},{6,5},{7,6},{8,7},{9,8},{10,9... | collective-permute-start | bytes 12296 | tf_op jit(solution)/shard_map/ppermute | solution.py:22
  92.1 0.7 copy.250
  92.8 1.3 %collective-permute-start.15 = (bf16[2,1,32,128]{3,1,2,0:T(2,128)(2,1)S(1)}, bf16[2,1,32,128]{3,1,2,0:T(2,128)(2,1)S(1)}, u32[]{:S(2)}, u32[]{:S(2)}) collective-permute-start(bf16[2,1,32,128]{3,1,2,0:T(2,128)(2,1)S(1)} %slice.650), channel_id=1, source_target_pairs={{8,0},{9,1},{10,2},{11,3},{12,4},{13,5},{14,6},{15,7},{24,16},{25,... | collective-permute-start | bytes 49160 | tf_op jit(solution)/shard_map/ppermute | solution.py:17
  94.1 5.4 %collective-permute-start.12 = (f32[1,1,32,128]{3,2,1,0:T(8,128)S(1)}, f32[1,1,32,128]{3,2,1,0:T(8,128)S(1)}, u32[]{:S(2)}, u32[]{:S(2)}) collective-permute-start(f32[1,1,32,128]{3,2,1,0:T(8,128)S(1)} %bitcast.411), channel_id=1, source_target_pairs={{0,8},{1,9},{2,10},{3,11},{4,12},{5,13},{6,14},{7,15},{16,24},{17,... | collective-permute-start | bytes 49160 | tf_op jit(solution)/shard_map/ppermute | solution.py:17
  100.0 1.0 %collective-permute-done.12 = f32[1,1,32,128]{3,2,1,0:T(8,128)S(1)} collective-permute-done((f32[1,1,32,128]{3,2,1,0:T(8,128)S(1)}, f32[1,1,32,128]{3,2,1,0:T(8,128)S(1)}, u32[]{:S(2)}, u32[]{:S(2)}) %collective-permute-start.12) | collective-permute-done | bytes 16416 | tf_op jit(solution)/shard_map/ppermute | solution.py:17
  101.8 0.9 multiply_subtract_fusion
  (217 shorter events, 28.6 us)
Async XLA Ops:
  0.6 12.9 %copy-start = (bf16[8,256]{1,0:T(8,128)(2,1)S(1)}, bf16[8,256]{1,0:T(8,128)(2,1)}, u32[]{:S(2)}) copy-start(bf16[8,256]{1,0:T(8,128)(2,1)} %param.28) | copy-start | bytes 12292
  0.6 21.7 %copy-start.2 = (f32[6,1,4,32,128]{4,3,2,1,0:T(8,128)S(1)}, f32[6,1,4,32,128]{4,3,2,1,0:T(8,128)}, u32[]{:S(2)}) copy-start(f32[6,1,4,32,128]{4,3,2,1,0:T(8,128)} %param.20) | copy-start | bytes 1179652
  1.4 40.9 %collective-permute-start = (bf16[1,1,32,128]{3,2,1,0:T(8,128)(2,1)S(1)}, bf16[1,1,32,128]{3,2,1,0:T(8,128)(2,1)S(1)}, u32[]{:S(2)}, u32[]{:S(2)}) collective-permute-start(bf16[1,1,32,128]{3,2,1,0:T(8,128)(2,1)S(1)} %slice.652), channel_id=1, source_target_pairs={{8,0},{9,1},{10,2},{11,3},{12,4},{13,5},{14,6},{15,7},{24,16},{25,... | collective-permute-start | bytes 24584 | tf_op jit(solution)/shard_map/ppermute | solution.py:17
  3.5 32.3 %collective-permute-start.1 = (f32[2,4,1,128]{3,2,1,0:T(1,128)S(1)}, f32[2,4,1,128]{3,2,1,0:T(1,128)S(1)}, u32[]{:S(2)}, u32[]{:S(2)}) collective-permute-start(f32[2,4,1,128]{3,2,1,0:T(1,128)S(1)} %slice.405), channel_id=1, source_target_pairs={{0,1},{1,2},{2,3},{3,4},{4,5},{5,6},{6,7},{7,8},{8,9},{9,10},{10,1... | collective-permute-start | bytes 12296 | tf_op jit(solution)/shard_map/ppermute | solution.py:22
  5.3 57.2 %collective-permute-start.2 = (f32[2,1,32,128]{3,2,1,0:T(8,128)}, f32[2,1,32,128]{3,2,1,0:T(8,128)}, u32[]{:S(2)}, u32[]{:S(2)}) collective-permute-start(f32[2,1,32,128]{3,2,1,0:T(8,128)} %slice.504), channel_id=1, source_target_pairs={{0,8},{1,9},{2,10},{3,11},{4,12},{5,13},{6,14},{7,15},{16,24},{17,... | collective-permute-start | bytes 98312 | tf_op jit(solution)/shard_map/ppermute | solution.py:17
  12.7 50.6 %collective-permute-start.3 = (f32[1,4,1,128]{3,2,1,0:T(1,128)}, f32[1,4,1,128]{3,2,1,0:T(1,128)}, u32[]{:S(2)}, u32[]{:S(2)}) collective-permute-start(f32[1,4,1,128]{3,2,1,0:T(1,128)} %slice.507), channel_id=1, source_target_pairs={{0,15},{1,0},{2,1},{3,2},{4,3},{5,4},{6,5},{7,6},{8,7},{9,8},{10,9... | collective-permute-start | bytes 6152 | tf_op jit(solution)/shard_map/ppermute | solution.py:22
  16.1 20.3 %all-to-all-start.2 = ((bf16[16,2,128]{2,1,0:T(2,128)(2,1)}), bf16[16,2,128]{2,1,0:T(2,128)(2,1)S(1)}, u32[]{:S(2)}, u32[]{:S(2)}) async-start(bf16[16,2,128]{2,1,0:T(2,128)(2,1)} %reshape.547), calls=%async_computation.2 | async-start | bytes 16384 | tf_op jit(solution)/shard_map/all_to_all | solution.py:95
  25.9 0.9 copy-start.17
  36.4 12.4 %all-to-all-start = ((bf16[16,2,128]{2,1,0:T(2,128)(2,1)}), bf16[16,2,128]{2,1,0:T(2,128)(2,1)S(1)}, u32[]{:S(2)}, u32[]{:S(2)}) async-start(bf16[16,2,128]{2,1,0:T(2,128)(2,1)} %reshape.543), calls=%async_computation | async-start | bytes 16384 | tf_op jit(solution)/shard_map/all_to_all | solution.py:96
  48.8 9.8 %all-to-all-start.1 = ((bf16[16,2,128]{2,1,0:T(2,128)(2,1)}), bf16[16,2,128]{2,1,0:T(2,128)(2,1)S(1)}, u32[]{:S(2)}, u32[]{:S(2)}) async-start(bf16[16,2,128]{2,1,0:T(2,128)(2,1)} %reshape.545), calls=%async_computation.1 | async-start | bytes 16384 | tf_op jit(solution)/shard_map/all_to_all | solution.py:94
  58.7 0.9 copy-start.18
  62.0 1.3 %copy-start.15 = (f32[4,31,128]{2,0,1:T(4,128)S(1)}, f32[4,31,128]{2,0,1:T(4,128)}, u32[]{:S(2)}) copy-start(f32[4,31,128]{2,0,1:T(4,128)} %slice.506) | copy-start | bytes 190468
  63.3 0.9 copy-start.8
  63.3 0.9 copy-start.10
  63.3 0.9 copy-start.13
  63.3 0.9 copy-start.14
  64.9 0.9 copy-start.3
  66.1 7.6 %collective-permute-start.6 = (f32[2,4,1,128]{3,1,2,0:T(4,128)S(1)}, f32[2,4,1,128]{3,1,2,0:T(4,128)S(1)}, u32[]{:S(2)}, u32[]{:S(2)}) collective-permute-start(f32[2,4,1,128]{3,1,2,0:T(4,128)S(1)} %slice.436), channel_id=1, source_target_pairs={{0,15},{1,0},{2,1},{3,2},{4,3},{5,4},{6,5},{7,6},{8,7},{9,8},{10,9... | collective-permute-start | bytes 12296 | tf_op jit(solution)/shard_map/ppermute | solution.py:22
  66.8 6.8 %collective-permute-start.7 = (bf16[2,1,32,128]{3,2,1,0:T(8,128)(2,1)S(1)}, bf16[2,1,32,128]{3,2,1,0:T(8,128)(2,1)S(1)}, u32[]{:S(2)}, u32[]{:S(2)}) collective-permute-start(bf16[2,1,32,128]{3,2,1,0:T(8,128)(2,1)S(1)} %copy.373), channel_id=1, source_target_pairs={{8,0},{9,1},{10,2},{11,3},{12,4},{13,5},{14,6},{15,7},{24,16},{25,... | collective-permute-start | bytes 49160 | tf_op jit(solution)/shard_map/ppermute | solution.py:17
  68.1 5.9 %collective-permute-start.5 = (f32[1,4,1,128]{3,1,2,0:T(4,128)S(1)}, f32[1,4,1,128]{3,1,2,0:T(4,128)S(1)}, u32[]{:S(2)}, u32[]{:S(2)}) collective-permute-start(f32[1,4,1,128]{3,1,2,0:T(4,128)S(1)} %slice.517), channel_id=1, source_target_pairs={{0,1},{1,2},{2,3},{3,4},{4,5},{5,6},{6,7},{7,8},{8,9},{9,10},{10,1... | collective-permute-start | bytes 6152 | tf_op jit(solution)/shard_map/ppermute | solution.py:22
  68.2 6.9 %collective-permute-start.4 = (f32[1,1,32,128]{3,1,2,0:T(1,128)S(1)}, f32[1,1,32,128]{3,1,2,0:T(1,128)S(1)}, u32[]{:S(2)}, u32[]{:S(2)}) collective-permute-start(f32[1,1,32,128]{3,1,2,0:T(1,128)S(1)} %slice.514), channel_id=1, source_target_pairs={{0,8},{1,9},{2,10},{3,11},{4,12},{5,13},{6,14},{7,15},{16,24},{17,... | collective-permute-start | bytes 49160 | tf_op jit(solution)/shard_map/ppermute | solution.py:17
  74.1 1.0 %copy-start.12 = (f32[1,4,32,128]{3,2,1,0:T(8,128)S(1)}, f32[1,4,32,128]{3,2,1,0:T(8,128)}, u32[]{:S(2)}) copy-start(f32[1,4,32,128]{3,2,1,0:T(8,128)} %param.22) | copy-start | bytes 196612
  75.4 1.0 copy-start.1
  77.7 7.6 %collective-permute-start.8 = (bf16[1,1,32,128]{3,2,1,0:T(8,128)(2,1)S(1)}, bf16[1,1,32,128]{3,2,1,0:T(8,128)(2,1)S(1)}, u32[]{:S(2)}, u32[]{:S(2)}) collective-permute-start(bf16[1,1,32,128]{3,2,1,0:T(8,128)(2,1)S(1)} %copy.396), channel_id=1, source_target_pairs={{8,0},{9,1},{10,2},{11,3},{12,4},{13,5},{14,6},{15,7},{24,16},{25,... | collective-permute-start | bytes 24584 | tf_op jit(solution)/shard_map/ppermute | solution.py:17
  79.0 6.3 %collective-permute-start.9 = (f32[2,4,1,128]{3,1,2,0:T(4,128)S(1)}, f32[2,4,1,128]{3,1,2,0:T(4,128)S(1)}, u32[]{:S(2)}, u32[]{:S(2)}) collective-permute-start(f32[2,4,1,128]{3,1,2,0:T(4,128)S(1)} %bitcast.419), channel_id=1, source_target_pairs={{0,1},{1,2},{2,3},{3,4},{4,5},{5,6},{6,7},{7,8},{8,9},{9,10},{10,1... | collective-permute-start | bytes 12296 | tf_op jit(solution)/shard_map/ppermute | solution.py:22
  79.5 6.7 %collective-permute-start.10 = (f32[2,1,32,128]{3,2,1,0:T(8,128)S(1)}, f32[2,1,32,128]{3,2,1,0:T(8,128)S(1)}, u32[]{:S(2)}, u32[]{:S(2)}) collective-permute-start(f32[2,1,32,128]{3,2,1,0:T(8,128)S(1)} %slice.541), channel_id=1, source_target_pairs={{0,8},{1,9},{2,10},{3,11},{4,12},{5,13},{6,14},{7,15},{16,24},{17,... | collective-permute-start | bytes 98312 | tf_op jit(solution)/shard_map/ppermute | solution.py:17
  85.2 1.4 %collective-permute-start.11 = (f32[1,4,1,128]{3,1,2,0:T(4,128)S(1)}, f32[1,4,1,128]{3,1,2,0:T(4,128)S(1)}, u32[]{:S(2)}, u32[]{:S(2)}) collective-permute-start(f32[1,4,1,128]{3,1,2,0:T(4,128)S(1)} %slice.546), channel_id=1, source_target_pairs={{0,15},{1,0},{2,1},{3,2},{4,3},{5,4},{6,5},{7,6},{8,7},{9,8},{10,9... | collective-permute-start | bytes 6152 | tf_op jit(solution)/shard_map/ppermute | solution.py:22
  87.2 12.3 %collective-permute-start.14 = (f32[2,4,1,128]{3,1,2,0:T(4,128)S(1)}, f32[2,4,1,128]{3,1,2,0:T(4,128)S(1)}, u32[]{:S(2)}, u32[]{:S(2)}) collective-permute-start(f32[2,4,1,128]{3,1,2,0:T(4,128)S(1)} %slice.486), channel_id=1, source_target_pairs={{0,15},{1,0},{2,1},{3,2},{4,3},{5,4},{6,5},{7,6},{8,7},{9,8},{10,9... | collective-permute-start | bytes 12296 | tf_op jit(solution)/shard_map/ppermute | solution.py:22
  92.8 6.8 %collective-permute-start.15 = (bf16[2,1,32,128]{3,1,2,0:T(2,128)(2,1)S(1)}, bf16[2,1,32,128]{3,1,2,0:T(2,128)(2,1)S(1)}, u32[]{:S(2)}, u32[]{:S(2)}) collective-permute-start(bf16[2,1,32,128]{3,1,2,0:T(2,128)(2,1)S(1)} %slice.650), channel_id=1, source_target_pairs={{8,0},{9,1},{10,2},{11,3},{12,4},{13,5},{14,6},{15,7},{24,16},{25,... | collective-permute-start | bytes 49160 | tf_op jit(solution)/shard_map/ppermute | solution.py:17
  94.0 5.9 %collective-permute-start.13 = (f32[1,4,1,128]{3,1,2,0:T(4,128)S(1)}, f32[1,4,1,128]{3,1,2,0:T(4,128)S(1)}, u32[]{:S(2)}, u32[]{:S(2)}) collective-permute-start(f32[1,4,1,128]{3,1,2,0:T(4,128)S(1)} %slice.559), channel_id=1, source_target_pairs={{0,1},{1,2},{2,3},{3,4},{4,5},{5,6},{6,7},{7,8},{8,9},{9,10},{10,1... | collective-permute-start | bytes 6152 | tf_op jit(solution)/shard_map/ppermute | solution.py:22
  94.1 6.9 %collective-permute-start.12 = (f32[1,1,32,128]{3,2,1,0:T(8,128)S(1)}, f32[1,1,32,128]{3,2,1,0:T(8,128)S(1)}, u32[]{:S(2)}, u32[]{:S(2)}) collective-permute-start(f32[1,1,32,128]{3,2,1,0:T(8,128)S(1)} %bitcast.411), channel_id=1, source_target_pairs={{0,8},{1,9},{2,10},{3,11},{4,12},{5,13},{6,14},{7,15},{16,24},{17,... | collective-permute-start | bytes 49160 | tf_op jit(solution)/shard_map/ppermute | solution.py:17
  101.8 0.9 copy-start.5
  (13 other events, 9.7 us)
where the time goes:
time: 104 us; the launch traced here: 103 us
  starting transfers between devices  49.3 us (47%)
  local copies, waits for them, and re-layouts  27.4 us (26%)
  waiting for transfers between devices  12.8 us (12%)
  other arithmetic  9.46 us (9%)
  matrix products  1.93 us (2%)
  between operations  1.82 us (2%)
    ppermute x8, starting transfers between devices, passed_along(): return lax.ppermute(block, axis, route)  27.3 us
    unnamed x91, local copies, waits for them, and re-layouts  11.2 us
    ppermute x8, starting transfers between devices, shifted(): lax.ppermute(array, axis, [(i, (i + by) % count) for i in range(count)])  7.12 us
    all_to_all x1, starting transfers between devices, body(): lax.all_to_all(pack(tile_buoy), 'gx', split_axis=0, concat_axis=0, tiled=...  6.01 us
    all_to_all x1, waiting for transfers between devices, body(): lax.all_to_all(pack(tile_buoy), 'gx', split_axis=0, concat_axis=0, tiled=...  5.65 us
    all_to_all x1, starting transfers between devices, body(): lax.all_to_all(pack(tile_mu), 'gx', split_axis=0, concat_axis=0, tiled=True)  5.46 us
    all_to_all x1, waiting for transfers between devices, body(): lax.all_to_all(pack(tile_lambda), 'gx', split_axis=0, concat_axis=0, tile...  3.85 us
    all_to_all x1, starting transfers between devices, body(): lax.all_to_all(pack(tile_lambda), 'gx', split_axis=0, concat_axis=0, tile...  3.42 us
  transfers between devices with their start and end apart: 19, of which 6 were waited for; matrix products, arithmetic and copies ran while one was open for 26% of the time, Pallas kernels for 0%

commit v1 on v0

v1 whole, which is shorter than its diff:
```python
import functools

import jax
import jax.numpy as jnp
from jax import lax
from jax.experimental import pallas as pl
from jax.experimental.pallas import tpu as pltpu
from jax.sharding import PartitionSpec as P

MESH = pl.DeviceIdType.MESH
F32 = jnp.float32
PY = 8
TY = 8
TZ = 8
COURANT = 0.25
UNROLL = 16


def each(count, body):
    if count <= UNROLL:
        for k in range(count):
            body(k)
    else:
        lax.fori_loop(0, count, lambda k, c: (body(k), c)[1], 0)


def kernel(
    n, steps,
    vel, stress, mem, lam, mu, buo, dec, los,
    tile_l, tile_m, tile_b, dest, bricks, index, wave,
    out_v, out_s, out_m,
    V, S, M, LAM, MU, BUO, DEC, LOS,
    packed, arrived, source,
    xa_send, xa_recv, xb_recv, ya_send, ya_recv, yb_send, yb_recv,
    load_sem, store_sem, tile_send, tile_recv, send_sem, recv_sem,
):
    me = lax.axis_index("gx")
    nx, ny, nz = LAM.shape
    per_device = tile_l.shape[0]
    has_ahead = me + PY < n
    has_behind = me >= PY
    next_y = lax.rem(me + 1, n)
    prev_y = lax.rem(me + n - 1, n)

    barrier = pltpu.get_barrier_semaphore()

    def greet(k):
        pl.semaphore_signal(
            barrier, inc=1, device_id={"gx": lax.rem(me + 1 + k, n)}, device_id_type=MESH
        )

    each(n - 1, greet)

    loads = [
        pltpu.make_async_copy(stress.at[:, 0], S.at[0], load_sem.at[0]),
        pltpu.make_async_copy(buo.at[0], BUO, load_sem.at[1]),
        pltpu.make_async_copy(vel.at[:, 0], V.at[0], load_sem.at[2]),
        pltpu.make_async_copy(lam.at[0], LAM, load_sem.at[3]),
        pltpu.make_async_copy(mu.at[0], MU, load_sem.at[4]),
        pltpu.make_async_copy(dec.at[0], DEC, load_sem.at[5]),
        pltpu.make_async_copy(los.at[0], LOS, load_sem.at[6]),
        pltpu.make_async_copy(mem.at[:, 0], M, load_sem.at[7]),
    ]
    for load in loads:
        load.start()

    rows = n * TZ
    row = lax.broadcasted_iota(jnp.int32, (rows, per_device), 0)
    chosen = (dest[...] == row // TZ).astype(F32)
    cells = tile_l.shape[1]
    wide_row = lax.broadcasted_iota(jnp.int32, (rows, cells), 0)
    wide_lane = lax.broadcasted_iota(jnp.int32, (rows, cells), 1)
    same = wide_row % TZ == wide_lane % TZ
    fold_row = lax.broadcasted_iota(jnp.int32, (cells, 128), 0) // TZ
    fold_lane = lax.broadcasted_iota(jnp.int32, (cells, 128), 1)
    total = jnp.zeros((rows, 128), F32)
    for prop, tiles in enumerate((tile_l, tile_m, tile_b)):
        spread = jnp.dot(chosen, tiles[...].astype(F32), preferred_element_type=F32)
        spread = jnp.where(same, spread, 0.0)
        fold = (fold_lane == fold_row + prop * nx * TY).astype(F32)
        total = total + jnp.dot(spread, fold, preferred_element_type=F32)
    packed[...] = total
    here = pl.ds(pl.multiple_of(me * TZ, TZ), TZ)
    arrived[here, :] = packed[here, :]

    @pl.when(jnp.logical_not(has_ahead))
    def _():
        xa_recv[...] = jnp.zeros_like(xa_recv)

    @pl.when(jnp.logical_not(has_behind))
    def _():
        xb_recv[...] = jnp.zeros_like(xb_recv)

    def copy_xa(r):
        count = 1 + r % 2
        return pltpu.make_async_remote_copy(
            xa_send.at[r, pl.ds(0, count)], xa_recv.at[r, pl.ds(0, count)],
            send_sem.at[r * 4], recv_sem.at[r * 4],
            device_id={"gx": lax.rem(me + n - PY, n)}, device_id_type=MESH,
        )

    def copy_xb(r):
        count = 2 - r % 2
        if r % 2 == 0:
            src = S.at[r // 2, pl.ds(3, 2), nx - 1]
        else:
            src = V.at[r // 2 + 1, pl.ds(0, 1), nx - 1]
        return pltpu.make_async_remote_copy(
            src, xb_recv.at[r, pl.ds(0, count)],
            send_sem.at[r * 4 + 1], recv_sem.at[r * 4 + 1],
            device_id={"gx": lax.rem(me + PY, n)}, device_id_type=MESH,
        )

    def copy_ya(r):
        return pltpu.make_async_remote_copy(
            ya_send.at[r], ya_recv.at[r], send_sem.at[r * 4 + 2], recv_sem.at[r * 4 + 2],
            device_id={"gx": prev_y}, device_id_type=MESH,
        )

    def copy_yb(r):
        return pltpu.make_async_remote_copy(
            yb_send.at[r], yb_recv.at[r], send_sem.at[r * 4 + 3], recv_sem.at[r * 4 + 3],
            device_id={"gx": next_y}, device_id_type=MESH,
        )

    def send_x_first(r, planes):
        for c, plane in enumerate(planes):
            xa_send[r, c] = plane.astype(jnp.bfloat16)
        pl.when(has_behind)(lambda: copy_xa(r).start())

    def send_x_last(r):
        pl.when(has_ahead)(lambda: copy_xb(r).start())

    def send_y(r, first, last):
        for c, (ref, comp) in enumerate(first):
            ya_send[r, c * nx:(c + 1) * nx, :] = ref[comp, :, 0, :]
        if len(first) == 1:
            ya_send[r, nx:, :] = jnp.zeros((8 - nx, nz), F32)
        for c, (ref, comp) in enumerate(last):
            yb_send[r, c * nx:(c + 1) * nx, :] = ref[comp, :, ny - 1, :]
        if len(last) == 1:
            yb_send[r, nx:, :] = jnp.zeros((8 - nx, nz), F32)
        copy_ya(r).start()
        copy_yb(r).start()

    def receive(r):
        copy_ya(r).wait_recv()
        copy_yb(r).wait_recv()
        pl.when(has_ahead)(lambda: copy_xa(r).wait_recv())
        pl.when(has_behind)(lambda: copy_xb(r).wait_recv())

    elems = index.shape[1]
    cell = index[...]
    where_row = (cell // nz).astype(F32)
    where_lane = (cell % nz).astype(F32)
    eye = lax.broadcasted_iota(jnp.int32, (elems, elems), 0) == lax.broadcasted_iota(
        jnp.int32, (elems, elems), 1
    )
    lane_of = jnp.sum(jnp.where(eye, where_lane, 0.0), axis=1, keepdims=True)
    on_row = (
        lax.broadcasted_iota(jnp.int32, (nx * ny, elems), 0).astype(F32) == where_row
    ).astype(F32)
    on_lane = lax.broadcasted_iota(jnp.int32, (elems, nz), 1).astype(F32) == lane_of
    for step in range(steps):
        amounts = jnp.where(on_lane, wave[:, step:step + 1], 0.0)
        source[step] = jnp.dot(
            on_row, amounts, preferred_element_type=F32, precision=lax.Precision.HIGHEST
        ).reshape(nx, ny, nz)

    spots = bricks.shape[1]
    width = spots * TZ
    owner = jnp.floor((bricks[...].astype(F32) + 0.5) * (1.0 / per_device))
    expand = (
        lax.broadcasted_iota(jnp.int32, (spots, width), 0)
        == lax.broadcasted_iota(jnp.int32, (spots, width), 1) // TZ
    ).astype(F32)
    owners = jnp.dot(
        jnp.broadcast_to(owner, (8, spots)), expand, preferred_element_type=F32
    )[0:1]
    live = owners >= 0.0
    place_row = lax.broadcasted_iota(jnp.int32, (rows, width), 0)
    place_lane = lax.broadcasted_iota(jnp.int32, (rows, width), 1)
    spread_to = (
        ((place_row // TZ).astype(F32) == owners) & (place_row % TZ == place_lane % TZ)
    ).astype(F32)

    loads[0].wait()
    pl.semaphore_wait(barrier, n - 1)

    send_x_last(0)
    send_x_first(0, [S[0, 0, 0]])

    def send_tiles(k):
        target = lax.rem(me + 1 + k, n)
        there = pl.ds(pl.multiple_of(target * TZ, TZ), TZ)
        pltpu.make_async_remote_copy(
            packed.at[there], arrived.at[here], tile_send, tile_recv,
            device_id={"gx": target}, device_id_type=MESH,
        ).start()

    each(n - 1, send_tiles)
    send_y(0, [(S.at[0], 1)], [(S.at[0], 3), (S.at[0], 5)])

    for load in loads[1:]:
        load.wait()

    part = pl.ds(0, (n - 1) * TZ)
    pltpu.make_async_copy(arrived.at[part], arrived.at[part], tile_recv).wait()
    placed = lax.dot_general(
        arrived[...].T, spread_to, (((1,), (0,)), ((), ())), preferred_element_type=F32
    )
    for prop, field in enumerate((LAM, MU, BUO)):
        for i in range(nx):
            for ry in range(ny // TY):
                top = (prop * nx + i) * TY
                piece = placed[top:top + TY, ry * nz:(ry + 1) * nz]
                at = slice(ry * TY, (ry + 1) * TY)
                field[i, at, :] = jnp.where(
                    live[:, ry * nz:(ry + 1) * nz], piece, field[i, at, :]
                )

    y_of = lax.broadcasted_iota(jnp.int32, (ny, nz), 0)
    z_of = lax.broadcasted_iota(jnp.int32, (ny, nz), 1)

    def after_y(a, halo):
        return jnp.where(y_of == ny - 1, halo, pltpu.roll(a, ny - 1, 0))

    def before_y(a, halo):
        return jnp.where(y_of == 0, halo, pltpu.roll(a, 1, 0))

    def after_z(a):
        return jnp.where(z_of == nz - 1, 0.0, pltpu.roll(a, nz - 1, 1))

    def before_z(a):
        return jnp.where(z_of == 0, 0.0, pltpu.roll(a, 1, 1))

    order = [0, nx - 1] + list(range(1, nx - 1))
    stores = []

    for step in range(steps):
        last = step == steps - 1
        r = 2 * step
        s, v_old, v = S.at[step], V.at[step], V.at[step + 1]
        receive(r)

        def row_of(buf, r, comp, i):
            at = comp * nx + i
            return buf[r, at:at + 1, :]

        for i in order:
            scale = COURANT * BUO[i]
            xy, xz, yz = s[3, i], s[4, i], s[5, i]
            ahead = s[0, i + 1] if i < nx - 1 else xa_recv[r, 0].astype(F32)
            gx = (
                (ahead - s[0, i])
                + (xy - before_y(xy, row_of(yb_recv, r, 0, i)))
                + (xz - before_z(xz))
            )
            behind = s[3, i - 1] if i > 0 else xb_recv[r, 0]
            yy = s[1, i]
            gy = (
                (xy - behind)
                + (after_y(yy, row_of(ya_recv, r, 0, i)) - yy)
                + (yz - before_z(yz))
            )
            behind = s[4, i - 1] if i > 0 else xb_recv[r, 1]
            zz = s[2, i]
            gz = (
                (xz - behind)
                + (yz - before_y(yz, row_of(yb_recv, r, 1, i)))
                + (after_z(zz) - zz)
            )
            v[0, i] = v_old[0, i] + scale * gx
            v[1, i] = v_old[1, i] + scale * gy
            v[2, i] = v_old[2, i] + scale * gz
            if i == 0:
                send_x_first(r + 1, [v[1, 0], v[2, 0]])
            if i == nx - 1:
                send_x_last(r + 1)
        send_y(r + 1, [(v, 0), (v, 2)], [(v, 1)])
        if last:
            stores.append(pltpu.make_async_copy(v, out_v.at[:, 0], store_sem.at[0]))
            stores[-1].start()

        r = r + 1
        receive(r)
        s_new = S.at[step + 1]
        for i in order:
            lame, shear = LAM[i], MU[i]
            vx, vy, vz = v[0, i], v[1, i], v[2, i]
            behind = v[0, i - 1] if i > 0 else xb_recv[r, 0]
            ex = vx - behind
            ey = vy - before_y(vy, row_of(yb_recv, r, 0, i))
            ez = vz - before_z(vz)
            spread = lame * (ex + ey + ez)
            ahead_y = v[1, i + 1] if i < nx - 1 else xa_recv[r, 0].astype(F32)
            ahead_z = v[2, i + 1] if i < nx - 1 else xa_recv[r, 1].astype(F32)
            rates = (
                spread + 2.0 * shear * ex,
                spread + 2.0 * shear * ey,
                spread + 2.0 * shear * ez,
                shear * ((after_y(vx, row_of(ya_recv, r, 0, i)) - vx) + (ahead_y - vy)),
                shear * ((after_z(vx) - vx) + (ahead_z - vz)),
                shear * ((after_z(vy) - vy) + (after_y(vz, row_of(ya_recv, r, 1, i)) - vz)),
            )
            keep = DEC[i]
            drop = (1.0 - keep) * LOS[i]
            for c in range(6):
                m = keep * M[c, i] - drop * rates[c]
                M[c, i] = m
                new = s[c, i] + COURANT * (rates[c] + m)
                s_new[c, i] = new + source[step, i] if c < 3 else new
            if last:
                k = 1 + 2 * i
                stores.append(
                    pltpu.make_async_copy(s_new.at[:, i], out_s.at[:, 0, i], store_sem.at[k])
                )
                stores[-1].start()
                stores.append(
                    pltpu.make_async_copy(M.at[:, i], out_m.at[:, 0, i], store_sem.at[k + 1])
                )
                stores[-1].start()
            else:
                if i == 0:
                    send_x_first(r + 1, [s_new[0, 0]])
                if i == nx - 1:
                    send_x_last(r + 1)
        if not last:
            send_y(r + 1, [(s_new, 1)], [(s_new, 3), (s_new, 5)])

    pltpu.make_async_copy(packed.at[part], packed.at[part], tile_send).wait()
    for r in range(2 * steps):
        copy_ya(r).wait_send()
        copy_yb(r).wait_send()
        pl.when(has_behind)(functools.partial(lambda q: copy_xa(q).wait_send(), r))
        pl.when(has_ahead)(functools.partial(lambda q: copy_xb(q).wait_send(), r))
    for store in stores:
        store.wait()


def body(n, velocity, stress, memory, lame_lambda, lame_mu, buoyancy, decay, loss,
         tile_lambda, tile_mu, tile_buoy, tile_dest, brick_tiles, src_index, src_wave):
    steps = src_wave.shape[1]
    grid = lame_lambda.shape[1:]
    nx, ny, nz = grid
    rounds = 2 * steps
    hbm = pl.BlockSpec(memory_space=pl.ANY)
    vmem = pl.BlockSpec(memory_space=pltpu.VMEM)
    big = (velocity, stress, memory, lame_lambda, lame_mu, buoyancy, decay, loss)
    return pl.pallas_call(
        functools.partial(kernel, n, steps),
        out_shape=tuple(
            jax.ShapeDtypeStruct(a.shape, F32) for a in (velocity, stress, memory)
        ),
        in_specs=[hbm] * len(big) + [vmem] * 7,
        out_specs=(hbm,) * 3,
        scratch_shapes=[
            pltpu.VMEM((steps + 1, 3) + grid, F32),
            pltpu.VMEM((steps + 1, 6) + grid, F32),
            pltpu.VMEM((6,) + grid, F32),
        ] + [pltpu.VMEM(grid, F32)] * 5 + [
            pltpu.VMEM((n * TZ, 128), F32),
            pltpu.VMEM((n * TZ, 128), F32),
            pltpu.VMEM((steps,) + grid, F32),
            pltpu.VMEM((rounds, 2, ny, nz), jnp.bfloat16),
            pltpu.VMEM((rounds, 2, ny, nz), jnp.bfloat16),
            pltpu.VMEM((rounds, 2, ny, nz), F32),
            pltpu.VMEM((rounds, 8, nz), F32),
            pltpu.VMEM((rounds, 8, nz), F32),
            pltpu.VMEM((rounds, 8, nz), F32),
            pltpu.VMEM((rounds, 8, nz), F32),
            pltpu.SemaphoreType.DMA((8,)),
            pltpu.SemaphoreType.DMA((1 + 2 * nx,)),
            pltpu.SemaphoreType.DMA,
            pltpu.SemaphoreType.DMA,
            pltpu.SemaphoreType.DMA((4 * rounds,)),
            pltpu.SemaphoreType.DMA((4 * rounds,)),
        ],
        compiler_params=pltpu.CompilerParams(
            collective_id=0, has_side_effects=True, vmem_limit_bytes=48 * 1024 * 1024
        ),
    )(
        *big, tile_lambda, tile_mu, tile_buoy, tile_dest.reshape(1, -1), brick_tiles,
        src_index.reshape(1, -1), src_wave,
    )


def solution(mesh):
    both = ("groups", "gx")
    field = P(None, both, None, None, None)
    single = P(both, None, None, None)
    return jax.shard_map(
        functools.partial(body, mesh.shape["gx"]),
        mesh=mesh,
        in_specs=(field,) * 3 + (single,) * 5 + (P(both, None),) * 3
        + (P(both), P(both, None), P(both), P(both, None)),
        out_specs=(field,) * 3,
        check_vma=False,
    )
```

time: 104 us -> 36.7 us (0.35)
  starting transfers between devices: 49.3 us -> 0 us
  Pallas kernels: 0 us -> 24.1 us
  local copies, waits for them, and re-layouts: 27.4 us -> 11.4 us
  waiting for transfers between devices: 12.8 us -> 0 us
  other arithmetic: 9.46 us -> 0 us
  matrix products: 1.93 us -> 0 us
  between operations: 1.82 us -> 0.7 us
    ppermute x16 -> x0, starting transfers between devices: 34.4 us -> none  [the longest x8 27.3 us: passed_along(): return lax.ppermute(block, axis, route)]
    pallas_call x0 -> x1, Pallas kernels: none -> 24.1 us  [body(): pl.pallas_call(functools.partial(kernel, n, steps), out_shape=tuple((jax....]
    all_to_all x3 -> x0, starting transfers between devices: 14.9 us -> none  [the longest x1 6.01 us: body(): lax.all_to_all(pack(tile_buoy), 'gx', split_axis=0, concat_axis=0, tiled=...]
    slice x47 -> x0, local copies, waits for them, and re-layouts: 9.94 us -> none  [the longest x8 1.62 us: forward_with(): rest = lax.slice_in_dim(values, 1, values.shape[along], axis=along)]
    all_to_all x3 -> x0, waiting for transfers between devices: 9.5 us -> none  [the longest x1 5.65 us: body(): lax.all_to_all(pack(tile_buoy), 'gx', split_axis=0, concat_axis=0, tiled=...]
    ppermute x16 -> x0, waiting for transfers between devices: 3.33 us -> none  [the longest x8 3.03 us: passed_along(): return lax.ppermute(block, axis, route)]
    add x15 -> x0, other arithmetic: 3.18 us -> none  [the longest x2 1 us: body(): backward_with(fields_s[3], behind_xs[0], 0)]
    reshape x6 -> x0, local copies, waits for them, and re-layouts: 2.69 us -> none  [place(): picked = picked.reshape(rows_y, rows_z, width_x, TY, TZ).transpose(2, 0,...]
  transfers between devices with their start and end apart: 19 -> 0, of which waited for: 6 -> 0; matrix products, arithmetic and copies ran while one was open for 26% -> 0% of each run, Pallas kernels for 0% -> 0%
where the time goes in v1:
time: 36.7 us; the launch traced here: 36.2 us
  Pallas kernels  24.1 us (66%)
  local copies, waits for them, and re-layouts  11.4 us (31%)
  between operations  0.7 us (2%)
    pallas_call x1, Pallas kernels, body(): pl.pallas_call(functools.partial(kernel, n, steps), out_shape=tuple((jax....  24.1 us
    unnamed x32, local copies, waits for them, and re-layouts  11.4 us

profile of v1, /device:TPU:0, one launch (start us, length us, event | category | flops | bytes accessed | tf_op | source)
XLA Modules:
  0.0 36.2 jit_solution(20413850813057765)
XLA Ops:
  0.6 0.0 copy-start.10
  0.6 0.0 copy-start.8
  0.7 0.0 copy-start.9
  0.7 0.0 copy-start.11
  0.7 0.8 %copy.18.wave = f32[16,2]{1,0:T(8,128)S(1)} copy(f32[16,2]{0,1:T(2,128)} %param.29) | data formatting | bytes 256 | tf_op args[14]
  1.5 0.0 copy-done.10
  1.5 0.0 copy-done.8
  1.5 0.0 copy-done.9
  1.5 0.0 copy-done.11
  1.5 0.0 copy-start
  1.5 1.0 %copy-done = f32[6,1,4,32,128]{4,3,2,1,0:T(8,128)S(1)} copy-done((f32[6,1,4,32,128]{4,3,2,1,0:T(8,128)S(1)}, f32[6,1,4,32,128]{4,3,2,1,0:T(8,128)}, u32[]{:S(2)}) %copy-start) | copy-done | bytes 393240
  2.5 0.0 copy-start.1
  2.5 1.0 %copy-done.1 = f32[6,1,4,32,128]{4,3,2,1,0:T(8,128)S(1)} copy-done((f32[6,1,4,32,128]{4,3,2,1,0:T(8,128)S(1)}, f32[6,1,4,32,128]{4,3,2,1,0:T(8,128)}, u32[]{:S(2)}) %copy-start.1) | copy-done | bytes 393240
  3.5 0.0 copy-start.2
  3.5 0.9 %copy-done.2 = f32[3,1,4,32,128]{4,3,2,1,0:T(8,128)S(1)} copy-done((f32[3,1,4,32,128]{4,3,2,1,0:T(8,128)S(1)}, f32[3,1,4,32,128]{4,3,2,1,0:T(8,128)}, u32[]{:S(2)}) %copy-start.2) | copy-done | bytes 196632
  4.4 0.0 copy-start.3
  4.4 0.8 %copy-done.3 = f32[1,4,32,128]{3,2,1,0:T(8,128)S(1)} copy-done((f32[1,4,32,128]{3,2,1,0:T(8,128)S(1)}, f32[1,4,32,128]{3,2,1,0:T(8,128)}, u32[]{:S(2)}) %copy-start.3) | copy-done | bytes 65560
  5.2 0.0 copy-start.4
  5.2 0.8 %copy-done.4 = f32[1,4,32,128]{3,2,1,0:T(8,128)S(1)} copy-done((f32[1,4,32,128]{3,2,1,0:T(8,128)S(1)}, f32[1,4,32,128]{3,2,1,0:T(8,128)}, u32[]{:S(2)}) %copy-start.4) | copy-done | bytes 65560
  6.1 0.0 copy-start.5
  6.1 0.8 %copy-done.5 = f32[1,4,32,128]{3,2,1,0:T(8,128)S(1)} copy-done((f32[1,4,32,128]{3,2,1,0:T(8,128)S(1)}, f32[1,4,32,128]{3,2,1,0:T(8,128)}, u32[]{:S(2)}) %copy-start.5) | copy-done | bytes 65560
  6.9 0.0 copy-start.6
  6.9 0.8 %copy-done.6 = f32[1,4,32,128]{3,2,1,0:T(8,128)S(1)} copy-done((f32[1,4,32,128]{3,2,1,0:T(8,128)S(1)}, f32[1,4,32,128]{3,2,1,0:T(8,128)}, u32[]{:S(2)}) %copy-start.6) | copy-done | bytes 65560
  7.8 0.0 copy-start.7
  7.8 0.8 %copy-done.7 = f32[1,4,32,128]{3,2,1,0:T(8,128)S(1)} copy-done((f32[1,4,32,128]{3,2,1,0:T(8,128)S(1)}, f32[1,4,32,128]{3,2,1,0:T(8,128)}, u32[]{:S(2)}) %copy-start.7) | copy-done | bytes 65560
  8.6 0.0 copy-start.12
  8.6 0.7 %copy-done.12 = s32[1,64]{1,0:T(1,128)S(1)} copy-done((s32[1,64]{1,0:T(1,128)S(1)}, s32[1,64]{1,0:T(1,128)}, u32[]{:S(2)}) %copy-start.12) | copy-done | bytes 280
  9.3 0.7 %copy-done.13 = s32[16]{0:T(128)S(1)} copy-done((s32[16]{0:T(128)S(1)}, s32[16]{0:T(128)}, u32[]{:S(2)}) %copy-start.13) | copy-done | bytes 88
  9.9 24.1 %shard_map.166 = (f32[3,1,4,32,128]{4,3,2,1,0:T(8,128)S(1)}, f32[6,1,4,32,128]{4,3,2,1,0:T(8,128)S(1)}, f32[6,1,4,32,128]{4,3,2,1,0:T(8,128)S(1)}) custom-call(f32[3,1,4,32,128]{4,3,2,1,0:T(8,128)S(1)} %copy-done.2, f32[6,1,4,32,128]{4,3,2,1,0:T(8,128)S(1)} %copy-done, f32[6,1,4,32,128]{4,3,2,1,0:T(8,128)S(1)} %copy-done.1, f32[1,4,32,128]{3,2,1,0:T(8,128)S(1)} %copy-done.3, ...), custom_call_target="tpu_custom_call" | custom-call | tf_op jit(solution)/shard_map/pallas_call | solution.py:350
  34.0 0.7 %copy.22 = f32[3,1,4,32,128]{4,3,2,1,0:T(8,128)} copy(f32[3,1,4,32,128]{4,3,2,1,0:T(8,128)S(1)} %get-tuple-element.6) | data formatting | bytes 393216
  34.7 0.7 %copy.23 = f32[6,1,4,32,128]{4,3,2,1,0:T(8,128)} copy(f32[6,1,4,32,128]{4,3,2,1,0:T(8,128)S(1)} %get-tuple-element.7) | data formatting | bytes 786432
  35.4 0.7 %copy.24 = f32[6,1,4,32,128]{4,3,2,1,0:T(8,128)} copy(f32[6,1,4,32,128]{4,3,2,1,0:T(8,128)S(1)} %get-tuple-element.8) | data formatting | bytes 786432
  (1 shorter events, 0.0 us)
Async XLA Ops:
  0.6 0.8 %copy-start.10 = (bf16[8,256]{1,0:T(8,128)(2,1)S(1)}, bf16[8,256]{1,0:T(8,128)(2,1)}, u32[]{:S(2)}) copy-start(bf16[8,256]{1,0:T(8,128)(2,1)} %tile_b.1) | copy-start | bytes 12292
  0.6 0.8 %copy-start.8 = (bf16[8,256]{1,0:T(8,128)(2,1)S(1)}, bf16[8,256]{1,0:T(8,128)(2,1)}, u32[]{:S(2)}) copy-start(bf16[8,256]{1,0:T(8,128)(2,1)} %tile_l.1) | copy-start | bytes 12292
  0.7 0.8 %copy-start.9 = (bf16[8,256]{1,0:T(8,128)(2,1)S(1)}, bf16[8,256]{1,0:T(8,128)(2,1)}, u32[]{:S(2)}) copy-start(bf16[8,256]{1,0:T(8,128)(2,1)} %tile_m.1) | copy-start | bytes 12292
  0.7 0.8 %copy-start.11 = (s32[8]{0:T(128)S(1)}, s32[8]{0:T(128)}, u32[]{:S(2)}) copy-start(s32[8]{0:T(128)} %param.26) | copy-start | bytes 100
  1.5 1.0 %copy-start = (f32[6,1,4,32,128]{4,3,2,1,0:T(8,128)S(1)}, f32[6,1,4,32,128]{4,3,2,1,0:T(8,128)}, u32[]{:S(2)}) copy-start(f32[6,1,4,32,128]{4,3,2,1,0:T(8,128)} %stress.1) | copy-start | bytes 1179652
  2.5 1.0 %copy-start.1 = (f32[6,1,4,32,128]{4,3,2,1,0:T(8,128)S(1)}, f32[6,1,4,32,128]{4,3,2,1,0:T(8,128)}, u32[]{:S(2)}) copy-start(f32[6,1,4,32,128]{4,3,2,1,0:T(8,128)} %mem.1) | copy-start | bytes 1179652
  3.5 0.9 %copy-start.2 = (f32[3,1,4,32,128]{4,3,2,1,0:T(8,128)S(1)}, f32[3,1,4,32,128]{4,3,2,1,0:T(8,128)}, u32[]{:S(2)}) copy-start(f32[3,1,4,32,128]{4,3,2,1,0:T(8,128)} %vel.1) | copy-start | bytes 589828
  4.4 0.8 %copy-start.3 = (f32[1,4,32,128]{3,2,1,0:T(8,128)S(1)}, f32[1,4,32,128]{3,2,1,0:T(8,128)}, u32[]{:S(2)}) copy-start(f32[1,4,32,128]{3,2,1,0:T(8,128)} %lam.1) | copy-start | bytes 196612
  5.2 0.8 %copy-start.4 = (f32[1,4,32,128]{3,2,1,0:T(8,128)S(1)}, f32[1,4,32,128]{3,2,1,0:T(8,128)}, u32[]{:S(2)}) copy-start(f32[1,4,32,128]{3,2,1,0:T(8,128)} %mu.1) | copy-start | bytes 196612
  6.1 0.8 %copy-start.5 = (f32[1,4,32,128]{3,2,1,0:T(8,128)S(1)}, f32[1,4,32,128]{3,2,1,0:T(8,128)}, u32[]{:S(2)}) copy-start(f32[1,4,32,128]{3,2,1,0:T(8,128)} %buo.1) | copy-start | bytes 196612
  6.9 0.8 %copy-start.6 = (f32[1,4,32,128]{3,2,1,0:T(8,128)S(1)}, f32[1,4,32,128]{3,2,1,0:T(8,128)}, u32[]{:S(2)}) copy-start(f32[1,4,32,128]{3,2,1,0:T(8,128)} %dec.1) | copy-start | bytes 196612
  7.8 0.8 %copy-start.7 = (f32[1,4,32,128]{3,2,1,0:T(8,128)S(1)}, f32[1,4,32,128]{3,2,1,0:T(8,128)}, u32[]{:S(2)}) copy-start(f32[1,4,32,128]{3,2,1,0:T(8,128)} %los.1) | copy-start | bytes 196612
  8.6 0.7 %copy-start.12 = (s32[1,64]{1,0:T(1,128)S(1)}, s32[1,64]{1,0:T(1,128)}, u32[]{:S(2)}) copy-start(s32[1,64]{1,0:T(1,128)} %bricks.1) | copy-start | bytes 772
  9.2 0.7 %copy-start.13 = (s32[16]{0:T(128)S(1)}, s32[16]{0:T(128)}, u32[]{:S(2)}) copy-start(s32[16]{0:T(128)} %param.28) | copy-start | bytes 196

commit v2 on v1

--- a/solution.py
+++ b/solution.py
@@ -14,6 +14,7 @@
 TZ = 8
 COURANT = 0.25
 UNROLL = 16
+VMEM_LIMIT = 64 * 1024 * 1024 - 1024 * 1024
 
 
 def each(count, body):
@@ -27,12 +28,13 @@
 def kernel(
     n, steps,
     vel, stress, mem, lam, mu, buo, dec, los,
+    tile_l_in, tile_m_in, tile_b_in, dest_in, bricks_in, index_in, wave_in,
+    last_v, last_s, last_m,
+    V, S, M, LAM, MU, BUO, DEC, LOS,
     tile_l, tile_m, tile_b, dest, bricks, index, wave,
-    out_v, out_s, out_m,
-    V, S, M, LAM, MU, BUO, DEC, LOS,
     packed, arrived, source,
     xa_send, xa_recv, xb_recv, ya_send, ya_recv, yb_send, yb_recv,
-    load_sem, store_sem, tile_send, tile_recv, send_sem, recv_sem,
+    load_sem, small_sem, tile_send, tile_recv, send_sem, recv_sem,
 ):
     me = lax.axis_index("gx")
     nx, ny, nz = LAM.shape
@@ -51,6 +53,15 @@
 
     each(n - 1, greet)
 
+    small = [
+        pltpu.make_async_copy(src, dst, small_sem.at[k])
+        for k, (src, dst) in enumerate((
+            (dest_in, dest), (tile_l_in, tile_l), (tile_m_in, tile_m), (tile_b_in, tile_b),
+            (bricks_in, bricks), (index_in, index), (wave_in, wave),
+        ))
+    ]
+    for load in small:
+        load.start()
     loads = [
         pltpu.make_async_copy(stress.at[:, 0], S.at[0], load_sem.at[0]),
         pltpu.make_async_copy(buo.at[0], BUO, load_sem.at[1]),
@@ -63,6 +74,9 @@
     ]
     for load in loads:
         load.start()
+
+    for load in small:
+        load.wait()
 
     rows = n * TZ
     row = lax.broadcasted_iota(jnp.int32, (rows, per_device), 0)
@@ -104,7 +118,8 @@
         if r % 2 == 0:
             src = S.at[r // 2, pl.ds(3, 2), nx - 1]
         else:
-            src = V.at[r // 2 + 1, pl.ds(0, 1), nx - 1]
+            v = last_v if r // 2 == steps - 1 else V.at[r // 2 + 1]
+            src = v.at[pl.ds(0, 1), nx - 1]
         return pltpu.make_async_remote_copy(
             src, xb_recv.at[r, pl.ds(0, count)],
             send_sem.at[r * 4 + 1], recv_sem.at[r * 4 + 1],
@@ -160,11 +175,13 @@
     on_row = (
         lax.broadcasted_iota(jnp.int32, (nx * ny, elems), 0).astype(F32) == where_row
     ).astype(F32)
-    on_lane = lax.broadcasted_iota(jnp.int32, (elems, nz), 1).astype(F32) == lane_of
+    on_lane = (
+        lax.broadcasted_iota(jnp.int32, (elems, nz), 1).astype(F32) == lane_of
+    ).astype(F32)
     for step in range(steps):
-        amounts = jnp.where(on_lane, wave[:, step:step + 1], 0.0)
+        amounts = on_row * wave[step:step + 1, :]
         source[step] = jnp.dot(
-            on_row, amounts, preferred_element_type=F32, precision=lax.Precision.HIGHEST
+            amounts, on_lane, preferred_element_type=F32, precision=lax.Precision.HIGHEST
         ).reshape(nx, ny, nz)
 
     spots = bricks.shape[1]
@@ -235,12 +252,13 @@
         return jnp.where(z_of == 0, 0.0, pltpu.roll(a, 1, 1))
 
     order = [0, nx - 1] + list(range(1, nx - 1))
-    stores = []
-
     for step in range(steps):
         last = step == steps - 1
         r = 2 * step
-        s, v_old, v = S.at[step], V.at[step], V.at[step + 1]
+        s, v_old = S.at[step], V.at[step]
+        v = last_v if last else V.at[step + 1]
+        s_new = last_s if last else S.at[step + 1]
+        m_new = last_m if last else M
         receive(r)
 
         def row_of(buf, r, comp, i):
@@ -278,13 +296,9 @@
             if i == nx - 1:
                 send_x_last(r + 1)
         send_y(r + 1, [(v, 0), (v, 2)], [(v, 1)])
-        if last:
-            stores.append(pltpu.make_async_copy(v, out_v.at[:, 0], store_sem.at[0]))
-            stores[-1].start()
 
         r = r + 1
         receive(r)
-        s_new = S.at[step + 1]
         for i in order:
             lame, shear = LAM[i], MU[i]
             vx, vy, vz = v[0, i], v[1, i], v[2, i]
@@ -307,24 +321,13 @@
             drop = (1.0 - keep) * LOS[i]
             for c in range(6):
                 m = keep * M[c, i] - drop * rates[c]
-                M[c, i] = m
+                m_new[c, i] = m
                 new = s[c, i] + COURANT * (rates[c] + m)
                 s_new[c, i] = new + source[step, i] if c < 3 else new
-            if last:
-                k = 1 + 2 * i
-                stores.append(
-                    pltpu.make_async_copy(s_new.at[:, i], out_s.at[:, 0, i], store_sem.at[k])
-                )
-                stores[-1].start()
-                stores.append(
-                    pltpu.make_async_copy(M.at[:, i], out_m.at[:, 0, i], store_sem.at[k + 1])
-                )
-                stores[-1].start()
-            else:
-                if i == 0:
-                    send_x_first(r + 1, [s_new[0, 0]])
-                if i == nx - 1:
-                    send_x_last(r + 1)
+            if not last and i == 0:
+                send_x_first(r + 1, [s_new[0, 0]])
+            if not last and i == nx - 1:
+                send_x_last(r + 1)
         if not last:
             send_y(r + 1, [(s_new, 1)], [(s_new, 3), (s_new, 5)])
 
@@ -334,6 +337,15 @@
         copy_yb(r).wait_send()
         pl.when(has_behind)(functools.partial(lambda q: copy_xa(q).wait_send(), r))
         pl.when(has_ahead)(functools.partial(lambda q: copy_xb(q).wait_send(), r))
+
+
+def write(v, s, m, out_v, out_s, out_m, sems):
+    stores = [
+        pltpu.make_async_copy(src, dst.at[:, 0], sems.at[k])
+        for k, (src, dst) in enumerate(((s, out_s), (m, out_m), (v, out_v)))
+    ]
+    for store in stores:
+        store.start()
     for store in stores:
         store.wait()
 
@@ -344,21 +356,21 @@
     grid = lame_lambda.shape[1:]
     nx, ny, nz = grid
     rounds = 2 * steps
-    hbm = pl.BlockSpec(memory_space=pl.ANY)
+    hbm = pl.BlockSpec(memory_space=pltpu.HBM)
     vmem = pl.BlockSpec(memory_space=pltpu.VMEM)
     big = (velocity, stress, memory, lame_lambda, lame_mu, buoyancy, decay, loss)
-    return pl.pallas_call(
+    small = (tile_lambda, tile_mu, tile_buoy, tile_dest.reshape(1, -1), brick_tiles,
+             src_index.reshape(1, -1), src_wave.T)
+    states = pl.pallas_call(
         functools.partial(kernel, n, steps),
-        out_shape=tuple(
-            jax.ShapeDtypeStruct(a.shape, F32) for a in (velocity, stress, memory)
-        ),
-        in_specs=[hbm] * len(big) + [vmem] * 7,
-        out_specs=(hbm,) * 3,
+        out_shape=tuple(jax.ShapeDtypeStruct((c,) + grid, F32) for c in (3, 6, 6)),
+        in_specs=[hbm] * (len(big) + len(small)),
+        out_specs=(vmem,) * 3,
         scratch_shapes=[
-            pltpu.VMEM((steps + 1, 3) + grid, F32),
-            pltpu.VMEM((steps + 1, 6) + grid, F32),
+            pltpu.VMEM((steps, 3) + grid, F32),
+            pltpu.VMEM((steps, 6) + grid, F32),
             pltpu.VMEM((6,) + grid, F32),
-        ] + [pltpu.VMEM(grid, F32)] * 5 + [
+        ] + [pltpu.VMEM(grid, F32)] * 5 + [pltpu.VMEM(a.shape, a.dtype) for a in small] + [
             pltpu.VMEM((n * TZ, 128), F32),
             pltpu.VMEM((n * TZ, 128), F32),
             pltpu.VMEM((steps,) + grid, F32),
@@ -370,19 +382,25 @@
             pltpu.VMEM((rounds, 8, nz), F32),
             pltpu.VMEM((rounds, 8, nz), F32),
             pltpu.SemaphoreType.DMA((8,)),
-            pltpu.SemaphoreType.DMA((1 + 2 * nx,)),
+            pltpu.SemaphoreType.DMA((len(small),)),
             pltpu.SemaphoreType.DMA,
             pltpu.SemaphoreType.DMA,
             pltpu.SemaphoreType.DMA((4 * rounds,)),
             pltpu.SemaphoreType.DMA((4 * rounds,)),
         ],
         compiler_params=pltpu.CompilerParams(
-            collective_id=0, has_side_effects=True, vmem_limit_bytes=48 * 1024 * 1024
+            collective_id=0, has_side_effects=True, vmem_limit_bytes=VMEM_LIMIT
         ),
-    )(
-        *big, tile_lambda, tile_mu, tile_buoy, tile_dest.reshape(1, -1), brick_tiles,
-        src_index.reshape(1, -1), src_wave,
-    )
+    )(*big, *small)
+    return pl.pallas_call(
+        write,
+        out_shape=tuple(
+            jax.ShapeDtypeStruct(a.shape, F32) for a in (velocity, stress, memory)
+        ),
+        in_specs=[pl.BlockSpec(memory_space=pl.ANY)] * 3,
+        out_specs=(hbm,) * 3,
+        scratch_shapes=[pltpu.SemaphoreType.DMA((3,))],
+    )(*states)
 
 
 def solution(mesh):

time: 36.7 us -> 56.4 us (1.54)
  Pallas kernels: 24.1 us -> 55.6 us
  local copies, waits for them, and re-layouts: 11.4 us -> 0 us
    pallas_call x0 -> x1, Pallas kernels: none -> 30.9 us  [body(): pl.pallas_call(write, out_shape=tuple((jax.ShapeDtypeStruct(a.shape, F32)...]
    unnamed x32 -> x0, local copies, waits for them, and re-layouts: 11.4 us -> none
    pallas_call x1, Pallas kernels: 24.1 us -> 24.7 us  [body(): pl.pallas_call(functools.partial(kernel, n, steps), out_shape=tuple((jax....]
where the time goes in v2:
time: 56.4 us; the launch traced here: 56.2 us
  Pallas kernels  55.6 us (99%)
  between operations  0.64 us (1%)
    pallas_call x1, Pallas kernels, body(): pl.pallas_call(write, out_shape=tuple((jax.ShapeDtypeStruct(a.shape, F32)...  30.9 us
    pallas_call x1, Pallas kernels, body(): pl.pallas_call(functools.partial(kernel, n, steps), out_shape=tuple((jax....  24.7 us

profile of v2, /device:TPU:0, one launch (start us, length us, event | category | flops | bytes accessed | tf_op | source)
XLA Modules:
  0.0 56.2 jit_solution(6206501694278610661)
XLA Ops:
  0.6 24.7 %shard_map.166 = (f32[3,4,32,128]{3,2,1,0:T(8,128)}, f32[6,4,32,128]{3,2,1,0:T(8,128)}, f32[6,4,32,128]{3,2,1,0:T(8,128)}) custom-call(f32[3,1,4,32,128]{4,3,2,1,0:T(8,128)} %vel.1, f32[6,1,4,32,128]{4,3,2,1,0:T(8,128)} %stress.1, f32[6,1,4,32,128]{4,3,2,1,0:T(8,128)} %mem.1, f32[1,4,32,128]{3,2,1,0:T(8,128)} %lam.1, f32[1,4,32,128]{3,2,1,0:T(8,128)} %mu.1, ...), custom_call_target="tpu_custom_call" | custom-call | tf_op jit(solution)/shard_map/pallas_call | solution.py:364
  25.3 30.9 %shard_map.167 = (f32[3,1,4,32,128]{4,3,2,1,0:T(8,128)}, f32[6,1,4,32,128]{4,3,2,1,0:T(8,128)}, f32[6,1,4,32,128]{4,3,2,1,0:T(8,128)}) custom-call(f32[3,4,32,128]{3,2,1,0:T(8,128)} %get-tuple-element.6.v, f32[6,4,32,128]{3,2,1,0:T(8,128)} %get-tuple-element.7.s, f32[6,4,32,128]{3,2,1,0:T(8,128)} %get-tuple-element.8.m), custom_call_target="tpu_custom_call" | custom-call | tf_op jit(solution)/shard_map/pallas_call | solution.py:395

commit v3 on v2

--- a/solution.py
+++ b/solution.py
@@ -397,7 +397,7 @@
         out_shape=tuple(
             jax.ShapeDtypeStruct(a.shape, F32) for a in (velocity, stress, memory)
         ),
-        in_specs=[pl.BlockSpec(memory_space=pl.ANY)] * 3,
+        in_specs=[vmem] * 3,
         out_specs=(hbm,) * 3,
         scratch_shapes=[pltpu.SemaphoreType.DMA((3,))],
     )(*states)

time: 56.4 us -> 27.7 us (0.49)
  Pallas kernels: 55.6 us -> 26.8 us
    pallas_call x1, Pallas kernels: 30.9 us -> 2.17 us  [body(): pl.pallas_call(write, out_shape=tuple((jax.ShapeDtypeStruct(a.shape, F32)...]
where the time goes in v3:
time: 27.7 us; the launch traced here: 27.5 us
  Pallas kernels  26.8 us (97%)
  between operations  0.64 us (2%)
    pallas_call x1, Pallas kernels, body(): pl.pallas_call(functools.partial(kernel, n, steps), out_shape=tuple((jax....  24.7 us
    pallas_call x1, Pallas kernels, body(): pl.pallas_call(write, out_shape=tuple((jax.ShapeDtypeStruct(a.shape, F32)...  2.17 us

profile of v3, /device:TPU:0, one launch (start us, length us, event | category | flops | bytes accessed | tf_op | source)
XLA Modules:
  0.0 27.5 jit_solution(7566561473741319141)
XLA Ops:
  0.6 24.7 %shard_map.166 = (f32[3,4,32,128]{3,2,1,0:T(8,128)}, f32[6,4,32,128]{3,2,1,0:T(8,128)}, f32[6,4,32,128]{3,2,1,0:T(8,128)}) custom-call(f32[3,1,4,32,128]{4,3,2,1,0:T(8,128)} %vel.1, f32[6,1,4,32,128]{4,3,2,1,0:T(8,128)} %stress.1, f32[6,1,4,32,128]{4,3,2,1,0:T(8,128)} %mem.1, f32[1,4,32,128]{3,2,1,0:T(8,128)} %lam.1, f32[1,4,32,128]{3,2,1,0:T(8,128)} %mu.1, ...), custom_call_target="tpu_custom_call" | custom-call | tf_op jit(solution)/shard_map/pallas_call | solution.py:364
  25.3 2.2 %shard_map.167 = (f32[3,1,4,32,128]{4,3,2,1,0:T(8,128)}, f32[6,1,4,32,128]{4,3,2,1,0:T(8,128)}, f32[6,1,4,32,128]{4,3,2,1,0:T(8,128)}) custom-call(f32[3,4,32,128]{3,2,1,0:T(8,128)} %get-tuple-element.6.v, f32[6,4,32,128]{3,2,1,0:T(8,128)} %get-tuple-element.7.s, f32[6,4,32,128]{3,2,1,0:T(8,128)} %get-tuple-element.8.m), custom_call_target="tpu_custom_call" | custom-call | tf_op jit(solution)/shard_map/pallas_call | solution.py:395

commit v4 on v3

--- a/solution.py
+++ b/solution.py
@@ -33,8 +33,10 @@
     V, S, M, LAM, MU, BUO, DEC, LOS,
     tile_l, tile_m, tile_b, dest, bricks, index, wave,
     packed, arrived, source,
-    xa_send, xa_recv, xb_recv, ya_send, ya_recv, yb_send, yb_recv,
+    xa_send, xa_recv, xb_send, xb_recv, ya_send, ya_recv, yb_send, yb_recv,
+    corner_send, corner_recv,
     load_sem, small_sem, tile_send, tile_recv, send_sem, recv_sem,
+    corner_send_sem, corner_recv_sem,
 ):
     me = lax.axis_index("gx")
     nx, ny, nz = LAM.shape
@@ -94,6 +96,8 @@
         fold = (fold_lane == fold_row + prop * nx * TY).astype(F32)
         total = total + jnp.dot(spread, fold, preferred_element_type=F32)
     packed[...] = total
+    ya_send[...] = jnp.zeros_like(ya_send)
+    yb_send[...] = jnp.zeros_like(yb_send)
     here = pl.ds(pl.multiple_of(me * TZ, TZ), TZ)
     arrived[here, :] = packed[here, :]
 
@@ -105,37 +109,35 @@
     def _():
         xb_recv[...] = jnp.zeros_like(xb_recv)
 
+    def copy(r, k, send, recv, target):
+        return pltpu.make_async_remote_copy(
+            send, recv, send_sem.at[r * 4 + k], recv_sem.at[r * 4 + k],
+            device_id={"gx": lax.rem(target + 2 * n, n)}, device_id_type=MESH,
+        )
+
     def copy_xa(r):
-        count = 1 + r % 2
+        part = pl.ds(0, (1, 2, 1, 3)[min(r, 3)])
+        return copy(r, 0, xa_send.at[r, part], xa_recv.at[r, part], me - PY)
+
+    def copy_xb(r):
+        part = pl.ds(0, (2, 1, 1, 3)[min(r, 3)])
+        return copy(r, 1, xb_send.at[r, part], xb_recv.at[r, part], me + PY)
+
+    def copy_ya(r):
+        part = pl.ds(0, 8 if r < 3 else 16)
+        return copy(r, 2, ya_send.at[r, part], ya_recv.at[r, part], me - 1)
+
+    def copy_yb(r):
+        part = pl.ds(0, 8 if r < 3 else 16)
+        return copy(r, 3, yb_send.at[r, part], yb_recv.at[r, part], me + 1)
+
+    def copy_corner(step, k):
+        at = (step - 1) * 4 + k
         return pltpu.make_async_remote_copy(
-            xa_send.at[r, pl.ds(0, count)], xa_recv.at[r, pl.ds(0, count)],
-            send_sem.at[r * 4], recv_sem.at[r * 4],
-            device_id={"gx": lax.rem(me + n - PY, n)}, device_id_type=MESH,
-        )
-
-    def copy_xb(r):
-        count = 2 - r % 2
-        if r % 2 == 0:
-            src = S.at[r // 2, pl.ds(3, 2), nx - 1]
-        else:
-            v = last_v if r // 2 == steps - 1 else V.at[r // 2 + 1]
-            src = v.at[pl.ds(0, 1), nx - 1]
-        return pltpu.make_async_remote_copy(
-            src, xb_recv.at[r, pl.ds(0, count)],
-            send_sem.at[r * 4 + 1], recv_sem.at[r * 4 + 1],
-            device_id={"gx": lax.rem(me + PY, n)}, device_id_type=MESH,
-        )
-
-    def copy_ya(r):
-        return pltpu.make_async_remote_copy(
-            ya_send.at[r], ya_recv.at[r], send_sem.at[r * 4 + 2], recv_sem.at[r * 4 + 2],
-            device_id={"gx": prev_y}, device_id_type=MESH,
-        )
-
-    def copy_yb(r):
-        return pltpu.make_async_remote_copy(
-            yb_send.at[r], yb_recv.at[r], send_sem.at[r * 4 + 3], recv_sem.at[r * 4 + 3],
-            device_id={"gx": next_y}, device_id_type=MESH,
+            corner_send.at[at], corner_recv.at[at],
+            corner_send_sem.at[at], corner_recv_sem.at[at],
+            device_id={"gx": lax.rem(me + n + (PY + 1, -PY - 1, 1 - PY, PY - 1)[k], n)},
+            device_id_type=MESH,
         )
 
     def send_x_first(r, planes):
@@ -143,18 +145,16 @@
             xa_send[r, c] = plane.astype(jnp.bfloat16)
         pl.when(has_behind)(lambda: copy_xa(r).start())
 
-    def send_x_last(r):
+    def send_x_last(r, planes):
+        for c, plane in enumerate(planes):
+            xb_send[r, c] = plane
         pl.when(has_ahead)(lambda: copy_xb(r).start())
 
     def send_y(r, first, last):
-        for c, (ref, comp) in enumerate(first):
-            ya_send[r, c * nx:(c + 1) * nx, :] = ref[comp, :, 0, :]
-        if len(first) == 1:
-            ya_send[r, nx:, :] = jnp.zeros((8 - nx, nz), F32)
-        for c, (ref, comp) in enumerate(last):
-            yb_send[r, c * nx:(c + 1) * nx, :] = ref[comp, :, ny - 1, :]
-        if len(last) == 1:
-            yb_send[r, nx:, :] = jnp.zeros((8 - nx, nz), F32)
+        for c, part in enumerate(first):
+            ya_send[r, c * nx:(c + 1) * nx, :] = part
+        for c, part in enumerate(last):
+            yb_send[r, c * nx:(c + 1) * nx, :] = part
         copy_ya(r).start()
         copy_yb(r).start()
 
@@ -204,7 +204,7 @@
     loads[0].wait()
     pl.semaphore_wait(barrier, n - 1)
 
-    send_x_last(0)
+    send_x_last(0, [S[0, 3, nx - 1], S[0, 4, nx - 1]])
     send_x_first(0, [S[0, 0, 0]])
 
     def send_tiles(k):
@@ -216,7 +216,7 @@
         ).start()
 
     each(n - 1, send_tiles)
-    send_y(0, [(S.at[0], 1)], [(S.at[0], 3), (S.at[0], 5)])
+    send_y(0, [S[0, 1, :, 0, :]], [S[0, 3, :, ny - 1, :], S[0, 5, :, ny - 1, :]])
 
     for load in loads[1:]:
         load.wait()
@@ -236,25 +236,77 @@
                     live[:, ry * nz:(ry + 1) * nz], piece, field[i, at, :]
                 )
 
-    y_of = lax.broadcasted_iota(jnp.int32, (ny, nz), 0)
-    z_of = lax.broadcasted_iota(jnp.int32, (ny, nz), 1)
-
     def after_y(a, halo):
+        y_of = lax.broadcasted_iota(jnp.int32, a.shape, 0)
         return jnp.where(y_of == ny - 1, halo, pltpu.roll(a, ny - 1, 0))
 
     def before_y(a, halo):
+        y_of = lax.broadcasted_iota(jnp.int32, a.shape, 0)
         return jnp.where(y_of == 0, halo, pltpu.roll(a, 1, 0))
 
     def after_z(a):
+        z_of = lax.broadcasted_iota(jnp.int32, a.shape, 1)
         return jnp.where(z_of == nz - 1, 0.0, pltpu.roll(a, nz - 1, 1))
 
     def before_z(a):
+        z_of = lax.broadcasted_iota(jnp.int32, a.shape, 1)
         return jnp.where(z_of == 0, 0.0, pltpu.roll(a, 1, 1))
+
+    def only_y(plane_row, y):
+        at = lax.broadcasted_iota(jnp.int32, (ny, nz), 0) == y
+        return jnp.where(at, plane_row, 0.0)
+
+    def only_x(one_row, x, allowed):
+        at = lax.broadcasted_iota(jnp.int32, (nx, nz), 0) == x
+        return jnp.where(at & allowed, one_row, 0.0)
+
+    zero_row = jnp.zeros((1, nz), F32)
+
+    def after_x(a):
+        return jnp.concatenate([a[1:], zero_row], axis=0)
+
+    def before_x(a):
+        return jnp.concatenate([zero_row, a[:-1]], axis=0)
+
+    def send_first_partial(r, s, v):
+        scale = COURANT * BUO[0]
+        xy, yy, xz, yz, zz = s[3, 0], s[1, 0], s[4, 0], s[5, 0], s[2, 0]
+        gy = xy + (after_y(yy, 0.0) - yy) + (yz - before_z(yz))
+        gz = xz + (yz - before_y(yz, 0.0)) + (after_z(zz) - zz)
+        send_x_first(r, [s[0, 0], v[1, 0] + scale * gy, v[2, 0] + scale * gz])
+
+    def send_last_partial(r, s, v):
+        e = nx - 1
+        xx, xy, xz = s[0, e], s[3, e], s[4, e]
+        gx = (xy - before_y(xy, 0.0)) - xx + (xz - before_z(xz))
+        send_x_last(r, [xy, xz, v[0, e] + COURANT * BUO[e] * gx])
+
+    def send_corners(step, s):
+        e = nx - 1
+        at = (step - 1) * 4
+        corner_send[at] = jnp.broadcast_to(s[3, e, ny - 1:, :], (8, nz))
+        corner_send[at + 1, 0:4, :] = jnp.broadcast_to(s[1, 0, 0:1, :], (4, nz))
+        corner_send[at + 1, 4:8, :] = jnp.broadcast_to(s[0, 0, 0:1, :], (4, nz))
+        corner_send[at + 2] = jnp.broadcast_to(s[5, 0, ny - 1:, :], (8, nz))
+        corner_send[at + 3] = jnp.broadcast_to(s[4, e, 0:1, :], (8, nz))
+        for k in range(4):
+            copy_corner(step, k).start()
+
+    def send_y_partial(r, s, v):
+        xx, yy, zz, xy, xz, yz = (s[c, :, 0, :] for c in range(6))
+        scale = COURANT * BUO[:, 0, :]
+        gx = (after_x(xx) - xx) + xy + (xz - before_z(xz))
+        gz = (xz - before_x(xz)) + yz + (after_z(zz) - zz)
+        first = [yy, v[0, :, 0, :] + scale * gx, v[2, :, 0, :] + scale * gz]
+        yy, xy, yz = (s[c, :, ny - 1, :] for c in (1, 3, 5))
+        gy = (xy - before_x(xy)) - yy + (yz - before_z(yz))
+        scale = COURANT * BUO[:, ny - 1, :]
+        send_y(r, first, [xy, yz, v[1, :, ny - 1, :] + scale * gy])
 
     order = [0, nx - 1] + list(range(1, nx - 1))
     for step in range(steps):
         last = step == steps - 1
-        r = 2 * step
+        r = 0 if step == 0 else step + 2
         s, v_old = S.at[step], V.at[step]
         v = last_v if last else V.at[step + 1]
         s_new = last_s if last else S.at[step + 1]
@@ -291,31 +343,66 @@
             v[0, i] = v_old[0, i] + scale * gx
             v[1, i] = v_old[1, i] + scale * gy
             v[2, i] = v_old[2, i] + scale * gz
-            if i == 0:
-                send_x_first(r + 1, [v[1, 0], v[2, 0]])
-            if i == nx - 1:
-                send_x_last(r + 1)
-        send_y(r + 1, [(v, 0), (v, 2)], [(v, 1)])
-
-        r = r + 1
-        receive(r)
+            if step == 0 and i == 0:
+                send_x_first(1, [v[1, 0], v[2, 0]])
+            if step == 0 and i == nx - 1:
+                send_x_last(1, [v[0, i]])
+        if step == 0:
+            send_y(1, [v[0, :, 0, :], v[2, :, 0, :]], [v[1, :, ny - 1, :]])
+            if not last:
+                send_x_first(2, [BUO[0]])
+                send_x_last(2, [BUO[nx - 1]])
+                send_y(2, [BUO[:, 0, :]], [BUO[:, ny - 1, :]])
+            receive(1)
+            v_behind_x = xb_recv[1, 0]
+            v_ahead_y, v_ahead_z = xa_recv[1, 0].astype(F32), xa_recv[1, 1].astype(F32)
+            v_after_x, v_after_z = ya_recv[1, 0:nx, :], ya_recv[1, nx:2 * nx, :]
+            v_before_y = yb_recv[1, 0:nx, :]
+        else:
+            if step == 1:
+                receive(2)
+            at = (step - 1) * 4
+            for k in range(4):
+                copy_corner(step, k).wait_recv()
+            c_xy = corner_recv[at, 0:1, :]
+            c_yy, c_xx = corner_recv[at + 1, 0:1, :], corner_recv[at + 1, 4:5, :]
+            c_yz = corner_recv[at + 2, 0:1, :]
+            c_xz = corner_recv[at + 3, 0:1, :]
+            e = nx - 1
+            scale = COURANT * xb_recv[2, 0]
+            v_behind_x = xb_recv[r, 2] + scale * (s[0, 0] - only_y(c_xy, 0))
+            scale = COURANT * xa_recv[2, 0].astype(F32)
+            v_ahead_y = xa_recv[r, 1].astype(F32) + scale * (only_y(c_yy, ny - 1) - s[3, e])
+            v_ahead_z = xa_recv[r, 2].astype(F32) - scale * (only_y(c_yz, 0) + s[4, e])
+            scale = COURANT * ya_recv[2, 0:nx, :]
+            v_after_x = ya_recv[r, nx:2 * nx, :] + scale * (
+                only_x(c_xx, e, next_y + PY < n) - s[3, :, ny - 1, :]
+            )
+            v_after_z = ya_recv[r, 2 * nx:3 * nx, :] - scale * (
+                only_x(c_xz, 0, next_y >= PY) + s[5, :, ny - 1, :]
+            )
+            scale = COURANT * yb_recv[2, 0:nx, :]
+            v_before_y = yb_recv[r, 2 * nx:3 * nx, :] + scale * (
+                s[1, :, 0, :] - only_x(c_xy, 0, prev_y >= PY)
+            )
+
         for i in order:
             lame, shear = LAM[i], MU[i]
             vx, vy, vz = v[0, i], v[1, i], v[2, i]
-            behind = v[0, i - 1] if i > 0 else xb_recv[r, 0]
+            behind = v[0, i - 1] if i > 0 else v_behind_x
             ex = vx - behind
-            ey = vy - before_y(vy, row_of(yb_recv, r, 0, i))
+            ey = vy - before_y(vy, v_before_y[i:i + 1])
             ez = vz - before_z(vz)
             spread = lame * (ex + ey + ez)
-            ahead_y = v[1, i + 1] if i < nx - 1 else xa_recv[r, 0].astype(F32)
-            ahead_z = v[2, i + 1] if i < nx - 1 else xa_recv[r, 1].astype(F32)
+            ahead_y = v[1, i + 1] if i < nx - 1 else v_ahead_y
+            ahead_z = v[2, i + 1] if i < nx - 1 else v_ahead_z
             rates = (
                 spread + 2.0 * shear * ex,
                 spread + 2.0 * shear * ey,
                 spread + 2.0 * shear * ez,
-                shear * ((after_y(vx, row_of(ya_recv, r, 0, i)) - vx) + (ahead_y - vy)),
+                shear * ((after_y(vx, v_after_x[i:i + 1]) - vx) + (ahead_y - vy)),
                 shear * ((after_z(vx) - vx) + (ahead_z - vz)),
-                shear * ((after_z(vy) - vy) + (after_y(vz, row_of(ya_recv, r, 1, i)) - vz)),
+                shear * ((after_z(vy) - vy) + (after_y(vz, v_after_z[i:i + 1]) - vz)),
             )
             keep = DEC[i]
             drop = (1.0 - keep) * LOS[i]
@@ -325,18 +412,22 @@
                 new = s[c, i] + COURANT * (rates[c] + m)
                 s_new[c, i] = new + source[step, i] if c < 3 else new
             if not last and i == 0:
-                send_x_first(r + 1, [s_new[0, 0]])
+                send_first_partial(step + 3, s_new, v)
             if not last and i == nx - 1:
-                send_x_last(r + 1)
+                send_last_partial(step + 3, s_new, v)
         if not last:
-            send_y(r + 1, [(s_new, 1)], [(s_new, 3), (s_new, 5)])
+            send_y_partial(step + 3, s_new, v)
+            send_corners(step + 1, s_new)
 
     pltpu.make_async_copy(packed.at[part], packed.at[part], tile_send).wait()
-    for r in range(2 * steps):
+    for r in range(2 + steps if steps > 1 else 2):
         copy_ya(r).wait_send()
         copy_yb(r).wait_send()
         pl.when(has_behind)(functools.partial(lambda q: copy_xa(q).wait_send(), r))
         pl.when(has_ahead)(functools.partial(lambda q: copy_xb(q).wait_send(), r))
+    for step in range(1, steps):
+        for k in range(4):
+            copy_corner(step, k).wait_send()
 
 
 def write(v, s, m, out_v, out_s, out_m, sems):
@@ -355,7 +446,8 @@
     steps = src_wave.shape[1]
     grid = lame_lambda.shape[1:]
     nx, ny, nz = grid
-    rounds = 2 * steps
+    rounds = 2 + steps
+    corners = 4 * max(steps - 1, 1)
     hbm = pl.BlockSpec(memory_space=pltpu.HBM)
     vmem = pl.BlockSpec(memory_space=pltpu.VMEM)
     big = (velocity, stress, memory, lame_lambda, lame_mu, buoyancy, decay, loss)
@@ -374,19 +466,20 @@
             pltpu.VMEM((n * TZ, 128), F32),
             pltpu.VMEM((n * TZ, 128), F32),
             pltpu.VMEM((steps,) + grid, F32),
-            pltpu.VMEM((rounds, 2, ny, nz), jnp.bfloat16),
-            pltpu.VMEM((rounds, 2, ny, nz), jnp.bfloat16),
-            pltpu.VMEM((rounds, 2, ny, nz), F32),
-            pltpu.VMEM((rounds, 8, nz), F32),
-            pltpu.VMEM((rounds, 8, nz), F32),
-            pltpu.VMEM((rounds, 8, nz), F32),
-            pltpu.VMEM((rounds, 8, nz), F32),
+            pltpu.VMEM((rounds, 3, ny, nz), jnp.bfloat16),
+            pltpu.VMEM((rounds, 3, ny, nz), jnp.bfloat16),
+            pltpu.VMEM((rounds, 3, ny, nz), F32),
+            pltpu.VMEM((rounds, 3, ny, nz), F32),
+        ] + [pltpu.VMEM((rounds, 16, nz), F32)] * 4
+        + [pltpu.VMEM((corners, 8, nz), F32)] * 2 + [
             pltpu.SemaphoreType.DMA((8,)),
             pltpu.SemaphoreType.DMA((len(small),)),
             pltpu.SemaphoreType.DMA,
             pltpu.SemaphoreType.DMA,
             pltpu.SemaphoreType.DMA((4 * rounds,)),
             pltpu.SemaphoreType.DMA((4 * rounds,)),
+            pltpu.SemaphoreType.DMA((corners,)),
+            pltpu.SemaphoreType.DMA((corners,)),
         ],
         compiler_params=pltpu.CompilerParams(
             collective_id=0, has_side_effects=True, vmem_limit_bytes=VMEM_LIMIT

time: 27.7 us -> 22.7 us (0.82)
  Pallas kernels: 26.8 us -> 21.9 us
    pallas_call x1, Pallas kernels: 24.7 us -> 19.7 us  [body(): pl.pallas_call(functools.partial(kernel, n, steps), out_shape=tuple((jax....]
where the time goes in v4:
time: 22.7 us; the launch traced here: 22.5 us
  Pallas kernels  21.9 us (96%)
  between operations  0.64 us (3%)
    pallas_call x1, Pallas kernels, body(): pl.pallas_call(functools.partial(kernel, n, steps), out_shape=tuple((jax....  19.7 us
    pallas_call x1, Pallas kernels, body(): pl.pallas_call(write, out_shape=tuple((jax.ShapeDtypeStruct(a.shape, F32)...  2.17 us

profile of v4, /device:TPU:0, one launch (start us, length us, event | category | flops | bytes accessed | tf_op | source)
XLA Modules:
  0.0 22.5 jit_solution(11174155965136342581)
XLA Ops:
  0.6 19.7 %shard_map.166 = (f32[3,4,32,128]{3,2,1,0:T(8,128)}, f32[6,4,32,128]{3,2,1,0:T(8,128)}, f32[6,4,32,128]{3,2,1,0:T(8,128)}) custom-call(f32[3,1,4,32,128]{4,3,2,1,0:T(8,128)} %vel.1, f32[6,1,4,32,128]{4,3,2,1,0:T(8,128)} %stress.1, f32[6,1,4,32,128]{4,3,2,1,0:T(8,128)} %mem.1, f32[1,4,32,128]{3,2,1,0:T(8,128)} %lam.1, f32[1,4,32,128]{3,2,1,0:T(8,128)} %mu.1, ...), custom_call_target="tpu_custom_call" | custom-call | tf_op jit(solution)/shard_map/pallas_call | solution.py:456
  20.4 2.2 %shard_map.167 = (f32[3,1,4,32,128]{4,3,2,1,0:T(8,128)}, f32[6,1,4,32,128]{4,3,2,1,0:T(8,128)}, f32[6,1,4,32,128]{4,3,2,1,0:T(8,128)}) custom-call(f32[3,4,32,128]{3,2,1,0:T(8,128)} %get-tuple-element.6.v, f32[6,4,32,128]{3,2,1,0:T(8,128)} %get-tuple-element.7.s, f32[6,4,32,128]{3,2,1,0:T(8,128)} %get-tuple-element.8.m), custom_call_target="tpu_custom_call" | custom-call | tf_op jit(solution)/shard_map/pallas_call | solution.py:488

commit v5 on v3

--- a/solution.py
+++ b/solution.py
@@ -33,8 +33,10 @@
     V, S, M, LAM, MU, BUO, DEC, LOS,
     tile_l, tile_m, tile_b, dest, bricks, index, wave,
     packed, arrived, source,
-    xa_send, xa_recv, xb_recv, ya_send, ya_recv, yb_send, yb_recv,
+    xa_send, xa_recv, xb_send, xb_recv, ya_send, ya_recv, yb_send, yb_recv,
+    corner_send, corner_recv, table_send, table_recv,
     load_sem, small_sem, tile_send, tile_recv, send_sem, recv_sem,
+    corner_send_sem, corner_recv_sem,
 ):
     me = lax.axis_index("gx")
     nx, ny, nz = LAM.shape
@@ -93,49 +95,74 @@
         spread = jnp.where(same, spread, 0.0)
         fold = (fold_lane == fold_row + prop * nx * TY).astype(F32)
         total = total + jnp.dot(spread, fold, preferred_element_type=F32)
+    there = row // TZ
+    is_tile = dest[...] >= 0
+    lanes = 3 * nx * TY
+    tile_row = lax.broadcasted_iota(jnp.int32, (cells, 128), 0) // TZ
+    for meant, fold in (
+        ((dest[...] + PY == there) & is_tile,
+         (tile_row - (nx - 1) * TY == fold_lane - lanes) & (tile_row >= (nx - 1) * TY)),
+        (dest[...] - PY == there,
+         (tile_row == fold_lane - (lanes + TY)) & (tile_row < TY)),
+        ((jnp.where(dest[...] == n - 1, 0, dest[...] + 1) == there) & is_tile,
+         (tile_row % TY == TY - 1) & (tile_row // TY == fold_lane - (lanes + 2 * TY))),
+        ((jnp.where(dest[...] == 0, n - 1, dest[...] - 1) == there) & is_tile,
+         (tile_row % TY == 0) & (tile_row // TY == fold_lane - (lanes + 2 * TY + nx))),
+    ):
+        spread = jnp.dot(meant.astype(F32), tile_b[...].astype(F32), preferred_element_type=F32)
+        spread = jnp.where(same, spread, 0.0)
+        total = total + jnp.dot(spread, fold.astype(F32), preferred_element_type=F32)
     packed[...] = total
+    ya_send[...] = jnp.zeros_like(ya_send)
+    yb_send[...] = jnp.zeros_like(yb_send)
     here = pl.ds(pl.multiple_of(me * TZ, TZ), TZ)
     arrived[here, :] = packed[here, :]
 
     @pl.when(jnp.logical_not(has_ahead))
     def _():
         xa_recv[...] = jnp.zeros_like(xa_recv)
+        table_recv[0] = jnp.full(table_recv.shape[1:], -1.0, F32)
 
     @pl.when(jnp.logical_not(has_behind))
     def _():
         xb_recv[...] = jnp.zeros_like(xb_recv)
+        table_recv[1] = jnp.full(table_recv.shape[1:], -1.0, F32)
+
+    def copy(k, send, recv, target):
+        return pltpu.make_async_remote_copy(
+            send, recv, send_sem.at[k], recv_sem.at[k],
+            device_id={"gx": lax.rem(target + 2 * n, n)}, device_id_type=MESH,
+        )
 
     def copy_xa(r):
-        count = 1 + r % 2
+        part = pl.ds(0, 6 if r == 0 else 3)
+        return copy(r * 4, xa_send.at[r, part], xa_recv.at[r, part], me - PY)
+
+    def copy_xb(r):
+        part = pl.ds(0, 5 if r == 0 else 3)
+        return copy(r * 4 + 1, xb_send.at[r, part], xb_recv.at[r, part], me + PY)
+
+    def copy_ya(r):
+        part = pl.ds(0, 32 if r == 0 else 16)
+        return copy(r * 4 + 2, ya_send.at[r, part], ya_recv.at[r, part], me - 1)
+
+    def copy_yb(r):
+        part = pl.ds(0, 32 if r == 0 else 16)
+        return copy(r * 4 + 3, yb_send.at[r, part], yb_recv.at[r, part], me + 1)
+
+    def copy_table_a():
+        return copy(4 * steps, table_send, table_recv.at[0], me - PY)
+
+    def copy_table_b():
+        return copy(4 * steps + 1, table_send, table_recv.at[1], me + PY)
+
+    def copy_corner(step, k):
+        at = step * 4 + k
         return pltpu.make_async_remote_copy(
-            xa_send.at[r, pl.ds(0, count)], xa_recv.at[r, pl.ds(0, count)],
-            send_sem.at[r * 4], recv_sem.at[r * 4],
-            device_id={"gx": lax.rem(me + n - PY, n)}, device_id_type=MESH,
-        )
-
-    def copy_xb(r):
-        count = 2 - r % 2
-        if r % 2 == 0:
-            src = S.at[r // 2, pl.ds(3, 2), nx - 1]
-        else:
-            v = last_v if r // 2 == steps - 1 else V.at[r // 2 + 1]
-            src = v.at[pl.ds(0, 1), nx - 1]
-        return pltpu.make_async_remote_copy(
-            src, xb_recv.at[r, pl.ds(0, count)],
-            send_sem.at[r * 4 + 1], recv_sem.at[r * 4 + 1],
-            device_id={"gx": lax.rem(me + PY, n)}, device_id_type=MESH,
-        )
-
-    def copy_ya(r):
-        return pltpu.make_async_remote_copy(
-            ya_send.at[r], ya_recv.at[r], send_sem.at[r * 4 + 2], recv_sem.at[r * 4 + 2],
-            device_id={"gx": prev_y}, device_id_type=MESH,
-        )
-
-    def copy_yb(r):
-        return pltpu.make_async_remote_copy(
-            yb_send.at[r], yb_recv.at[r], send_sem.at[r * 4 + 3], recv_sem.at[r * 4 + 3],
-            device_id={"gx": next_y}, device_id_type=MESH,
+            corner_send.at[at], corner_recv.at[at],
+            corner_send_sem.at[at], corner_recv_sem.at[at],
+            device_id={"gx": lax.rem(me + n + (PY + 1, -PY - 1, 1 - PY, PY - 1)[k], n)},
+            device_id_type=MESH,
         )
 
     def send_x_first(r, planes):
@@ -143,18 +170,16 @@
             xa_send[r, c] = plane.astype(jnp.bfloat16)
         pl.when(has_behind)(lambda: copy_xa(r).start())
 
-    def send_x_last(r):
+    def send_x_last(r, planes):
+        for c, plane in enumerate(planes):
+            xb_send[r, c] = plane
         pl.when(has_ahead)(lambda: copy_xb(r).start())
 
     def send_y(r, first, last):
-        for c, (ref, comp) in enumerate(first):
-            ya_send[r, c * nx:(c + 1) * nx, :] = ref[comp, :, 0, :]
-        if len(first) == 1:
-            ya_send[r, nx:, :] = jnp.zeros((8 - nx, nz), F32)
-        for c, (ref, comp) in enumerate(last):
-            yb_send[r, c * nx:(c + 1) * nx, :] = ref[comp, :, ny - 1, :]
-        if len(last) == 1:
-            yb_send[r, nx:, :] = jnp.zeros((8 - nx, nz), F32)
+        for c, part in enumerate(first):
+            ya_send[r, c * nx:c * nx + part.shape[0], :] = part
+        for c, part in enumerate(last):
+            yb_send[r, c * nx:c * nx + part.shape[0], :] = part
         copy_ya(r).start()
         copy_yb(r).start()
 
@@ -163,6 +188,90 @@
         copy_yb(r).wait_recv()
         pl.when(has_ahead)(lambda: copy_xa(r).wait_recv())
         pl.when(has_behind)(lambda: copy_xb(r).wait_recv())
+
+    def after_y(a, halo):
+        y_of = lax.broadcasted_iota(jnp.int32, a.shape, 0)
+        return jnp.where(y_of == ny - 1, halo, pltpu.roll(a, ny - 1, 0))
+
+    def before_y(a, halo):
+        y_of = lax.broadcasted_iota(jnp.int32, a.shape, 0)
+        return jnp.where(y_of == 0, halo, pltpu.roll(a, 1, 0))
+
+    def after_z(a):
+        z_of = lax.broadcasted_iota(jnp.int32, a.shape, 1)
+        return jnp.where(z_of == nz - 1, 0.0, pltpu.roll(a, nz - 1, 1))
+
+    def before_z(a):
+        z_of = lax.broadcasted_iota(jnp.int32, a.shape, 1)
+        return jnp.where(z_of == 0, 0.0, pltpu.roll(a, 1, 1))
+
+    def only_y(plane_row, y):
+        at = lax.broadcasted_iota(jnp.int32, (ny, nz), 0) == y
+        return jnp.where(at, plane_row, 0.0)
+
+    def only_x(one_row, x, allowed):
+        at = lax.broadcasted_iota(jnp.int32, (nx, nz), 0) == x
+        return jnp.where(at & allowed, one_row, 0.0)
+
+    zero_row = jnp.zeros((1, nz), F32)
+
+    def after_x(a):
+        return jnp.concatenate([a[1:], zero_row], axis=0)
+
+    def before_x(a):
+        return jnp.concatenate([zero_row, a[:-1]], axis=0)
+
+    def send_first_partial(r, s, v):
+        scale = COURANT * BUO[0]
+        xy, yy, xz, yz, zz = s[3, 0], s[1, 0], s[4, 0], s[5, 0], s[2, 0]
+        gy = xy + (after_y(yy, 0.0) - yy) + (yz - before_z(yz))
+        gz = xz + (yz - before_y(yz, 0.0)) + (after_z(zz) - zz)
+        if r == 0:
+            send_x_first(r, [s[0, 0], v[1, 0], v[2, 0], gy, gz, BUO[0]])
+        else:
+            send_x_first(r, [s[0, 0], v[1, 0] + scale * gy, v[2, 0] + scale * gz])
+
+    def send_last_partial(r, s, v):
+        e = nx - 1
+        xx, xy, xz = s[0, e], s[3, e], s[4, e]
+        gx = (xy - before_y(xy, 0.0)) - xx + (xz - before_z(xz))
+        if r == 0:
+            send_x_last(r, [xy, xz, v[0, e], gx, BUO[e]])
+        else:
+            send_x_last(r, [xy, xz, v[0, e] + COURANT * BUO[e] * gx])
+
+    def send_corners(step, s):
+        e = nx - 1
+        at = step * 4
+        corner_send[at] = jnp.broadcast_to(s[3, e, ny - 1:, :], (8, nz))
+        corner_send[at + 1, 0:4, :] = jnp.broadcast_to(s[1, 0, 0:1, :], (4, nz))
+        corner_send[at + 1, 4:8, :] = jnp.broadcast_to(s[0, 0, 0:1, :], (4, nz))
+        corner_send[at + 2] = jnp.broadcast_to(s[5, 0, ny - 1:, :], (8, nz))
+        corner_send[at + 3] = jnp.broadcast_to(s[4, e, 0:1, :], (8, nz))
+        for k in range(4):
+            copy_corner(step, k).start()
+
+    def send_y_partial(r, s, v):
+        xx, yy, zz, xy, xz, yz = (s[c, :, 0, :] for c in range(6))
+        scale = COURANT * BUO[:, 0, :]
+        gx = (after_x(xx) - xx) + xy + (xz - before_z(xz))
+        gz = (xz - before_x(xz)) + yz + (after_z(zz) - zz)
+        buoy = BUO[:, 0, :]
+        vx, vz = v[0, :, 0, :], v[2, :, 0, :]
+        if r == 0:
+            first = [yy, vx, vz, gx, gz, buoy, table_send[0:1, :]]
+        else:
+            first = [yy, vx + scale * gx, vz + scale * gz]
+        yy, xy, yz = (s[c, :, ny - 1, :] for c in (1, 3, 5))
+        gy = (xy - before_x(xy)) - yy + (yz - before_z(yz))
+        buoy = BUO[:, ny - 1, :]
+        vy = v[1, :, ny - 1, :]
+        if r == 0:
+            bands = ny // TY
+            last = [xy, yz, vy, gy, buoy, table_send[bands - 1:bands, :]]
+        else:
+            last = [xy, yz, vy + COURANT * buoy * gy]
+        send_y(r, first, last)
 
     elems = index.shape[1]
     cell = index[...]
@@ -201,11 +310,17 @@
         ((place_row // TZ).astype(F32) == owners) & (place_row % TZ == place_lane % TZ)
     ).astype(F32)
 
-    loads[0].wait()
+    table_send[...] = jnp.zeros_like(table_send)
+    for ry in range(ny // TY):
+        table_send[ry:ry + 1, :] = owners[:, ry * nz:(ry + 1) * nz]
+    for load in loads[:3]:
+        load.wait()
     pl.semaphore_wait(barrier, n - 1)
 
-    send_x_last(0)
-    send_x_first(0, [S[0, 0, 0]])
+    send_last_partial(0, S.at[0], V.at[0])
+    send_first_partial(0, S.at[0], V.at[0])
+    pl.when(has_behind)(lambda: copy_table_a().start())
+    pl.when(has_ahead)(lambda: copy_table_b().start())
 
     def send_tiles(k):
         target = lax.rem(me + 1 + k, n)
@@ -216,15 +331,17 @@
         ).start()
 
     each(n - 1, send_tiles)
-    send_y(0, [(S.at[0], 1)], [(S.at[0], 3), (S.at[0], 5)])
-
-    for load in loads[1:]:
+    send_y_partial(0, S.at[0], V.at[0])
+    send_corners(0, S.at[0])
+
+    for load in loads[3:]:
         load.wait()
 
     part = pl.ds(0, (n - 1) * TZ)
     pltpu.make_async_copy(arrived.at[part], arrived.at[part], tile_recv).wait()
+    got = arrived[...].T
     placed = lax.dot_general(
-        arrived[...].T, spread_to, (((1,), (0,)), ((), ())), preferred_element_type=F32
+        got, spread_to, (((1,), (0,)), ((), ())), preferred_element_type=F32
     )
     for prop, field in enumerate((LAM, MU, BUO)):
         for i in range(nx):
@@ -236,30 +353,46 @@
                     live[:, ry * nz:(ry + 1) * nz], piece, field[i, at, :]
                 )
 
-    y_of = lax.broadcasted_iota(jnp.int32, (ny, nz), 0)
-    z_of = lax.broadcasted_iota(jnp.int32, (ny, nz), 1)
-
-    def after_y(a, halo):
-        return jnp.where(y_of == ny - 1, halo, pltpu.roll(a, ny - 1, 0))
-
-    def before_y(a, halo):
-        return jnp.where(y_of == 0, halo, pltpu.roll(a, 1, 0))
-
-    def after_z(a):
-        return jnp.where(z_of == nz - 1, 0.0, pltpu.roll(a, nz - 1, 1))
-
-    def before_z(a):
-        return jnp.where(z_of == 0, 0.0, pltpu.roll(a, 1, 1))
+    near_row = lax.broadcasted_iota(jnp.int32, (rows, nz), 0)
+    near_lane = lax.broadcasted_iota(jnp.int32, (rows, nz), 1)
+    near_same = near_row % TZ == near_lane % TZ
+    near_brick = (near_row // TZ).astype(F32)
+
+    def near(top, table, background):
+        where_to = ((near_brick == table) & near_same).astype(F32)
+        piece = jnp.dot(got[top:top + 8], where_to, preferred_element_type=F32)
+        return jnp.where(table >= 0.0, piece, background)
+
+    receive(0)
+    pl.when(has_ahead)(lambda: copy_table_a().wait_recv())
+    pl.when(has_behind)(lambda: copy_table_b().wait_recv())
+    behind_parts, ahead_parts = [], []
+    for ry in range(ny // TY):
+        at = slice(ry * TY, (ry + 1) * TY)
+        behind_parts.append(near(lanes, table_recv[1, ry:ry + 1, :], xb_recv[0, 4, at, :]))
+        ahead_parts.append(
+            near(lanes + TY, table_recv[0, ry:ry + 1, :], xa_recv[0, 5].astype(F32)[at])
+        )
+    scale_behind = COURANT * jnp.concatenate(behind_parts, axis=0)
+    scale_ahead = COURANT * jnp.concatenate(ahead_parts, axis=0)
+    both = jnp.concatenate(
+        [yb_recv[0, 4 * nx:5 * nx, :], ya_recv[0, 5 * nx:6 * nx, :]], axis=0
+    )
+    scale_before = COURANT * near(lanes + 2 * TY, yb_recv[0, 5 * nx:5 * nx + 1, :], both)[0:nx]
+    scale_after = COURANT * near(
+        lanes + 2 * TY, ya_recv[0, 6 * nx:6 * nx + 1, :], both
+    )[nx:2 * nx]
 
     order = [0, nx - 1] + list(range(1, nx - 1))
     for step in range(steps):
         last = step == steps - 1
-        r = 2 * step
+        r = step
         s, v_old = S.at[step], V.at[step]
         v = last_v if last else V.at[step + 1]
         s_new = last_s if last else S.at[step + 1]
         m_new = last_m if last else M
-        receive(r)
+        if step > 0:
+            receive(r)
 
         def row_of(buf, r, comp, i):
             at = comp * nx + i
@@ -291,31 +424,57 @@
             v[0, i] = v_old[0, i] + scale * gx
             v[1, i] = v_old[1, i] + scale * gy
             v[2, i] = v_old[2, i] + scale * gz
-            if i == 0:
-                send_x_first(r + 1, [v[1, 0], v[2, 0]])
-            if i == nx - 1:
-                send_x_last(r + 1)
-        send_y(r + 1, [(v, 0), (v, 2)], [(v, 1)])
-
-        r = r + 1
-        receive(r)
+        at = step * 4
+        for k in range(4):
+            copy_corner(step, k).wait_recv()
+        c_xy = corner_recv[at, 0:1, :]
+        c_yy, c_xx = corner_recv[at + 1, 0:1, :], corner_recv[at + 1, 4:5, :]
+        c_yz = corner_recv[at + 2, 0:1, :]
+        c_xz = corner_recv[at + 3, 0:1, :]
+        e = nx - 1
+        rows_of = lambda buf, c: buf[r, c * nx:(c + 1) * nx, :]
+        if step == 0:
+            v_behind_x = xb_recv[r, 2] + scale_behind * xb_recv[r, 3]
+            v_ahead_y = xa_recv[r, 1].astype(F32) + scale_ahead * xa_recv[r, 3].astype(F32)
+            v_ahead_z = xa_recv[r, 2].astype(F32) + scale_ahead * xa_recv[r, 4].astype(F32)
+            v_after_x = rows_of(ya_recv, 1) + scale_after * rows_of(ya_recv, 3)
+            v_after_z = rows_of(ya_recv, 2) + scale_after * rows_of(ya_recv, 4)
+            v_before_y = rows_of(yb_recv, 2) + scale_before * rows_of(yb_recv, 3)
+        else:
+            v_behind_x = xb_recv[r, 2]
+            v_ahead_y, v_ahead_z = xa_recv[r, 1].astype(F32), xa_recv[r, 2].astype(F32)
+            v_after_x, v_after_z = rows_of(ya_recv, 1), rows_of(ya_recv, 2)
+            v_before_y = rows_of(yb_recv, 2)
+        v_behind_x = v_behind_x + scale_behind * (s[0, 0] - only_y(c_xy, 0))
+        v_ahead_y = v_ahead_y + scale_ahead * (only_y(c_yy, ny - 1) - s[3, e])
+        v_ahead_z = v_ahead_z - scale_ahead * (only_y(c_yz, 0) + s[4, e])
+        v_after_x = v_after_x + scale_after * (
+            only_x(c_xx, e, next_y + PY < n) - s[3, :, ny - 1, :]
+        )
+        v_after_z = v_after_z - scale_after * (
+            only_x(c_xz, 0, next_y >= PY) + s[5, :, ny - 1, :]
+        )
+        v_before_y = v_before_y + scale_before * (
+            s[1, :, 0, :] - only_x(c_xy, 0, prev_y >= PY)
+        )
+
         for i in order:
             lame, shear = LAM[i], MU[i]
             vx, vy, vz = v[0, i], v[1, i], v[2, i]
-            behind = v[0, i - 1] if i > 0 else xb_recv[r, 0]
+            behind = v[0, i - 1] if i > 0 else v_behind_x
             ex = vx - behind
-            ey = vy - before_y(vy, row_of(yb_recv, r, 0, i))
+            ey = vy - before_y(vy, v_before_y[i:i + 1])
             ez = vz - before_z(vz)
             spread = lame * (ex + ey + ez)
-            ahead_y = v[1, i + 1] if i < nx - 1 else xa_recv[r, 0].astype(F32)
-            ahead_z = v[2, i + 1] if i < nx - 1 else xa_recv[r, 1].astype(F32)
+            ahead_y = v[1, i + 1] if i < nx - 1 else v_ahead_y
+            ahead_z = v[2, i + 1] if i < nx - 1 else v_ahead_z
             rates = (
                 spread + 2.0 * shear * ex,
                 spread + 2.0 * shear * ey,
                 spread + 2.0 * shear * ez,
-                shear * ((after_y(vx, row_of(ya_recv, r, 0, i)) - vx) + (ahead_y - vy)),
+                shear * ((after_y(vx, v_after_x[i:i + 1]) - vx) + (ahead_y - vy)),
                 shear * ((after_z(vx) - vx) + (ahead_z - vz)),
-                shear * ((after_z(vy) - vy) + (after_y(vz, row_of(ya_recv, r, 1, i)) - vz)),
+                shear * ((after_z(vy) - vy) + (after_y(vz, v_after_z[i:i + 1]) - vz)),
             )
             keep = DEC[i]
             drop = (1.0 - keep) * LOS[i]
@@ -325,18 +484,24 @@
                 new = s[c, i] + COURANT * (rates[c] + m)
                 s_new[c, i] = new + source[step, i] if c < 3 else new
             if not last and i == 0:
-                send_x_first(r + 1, [s_new[0, 0]])
+                send_first_partial(step + 1, s_new, v)
             if not last and i == nx - 1:
-                send_x_last(r + 1)
+                send_last_partial(step + 1, s_new, v)
         if not last:
-            send_y(r + 1, [(s_new, 1)], [(s_new, 3), (s_new, 5)])
+            send_y_partial(step + 1, s_new, v)
+            send_corners(step + 1, s_new)
 
     pltpu.make_async_copy(packed.at[part], packed.at[part], tile_send).wait()
-    for r in range(2 * steps):
+    pl.when(has_behind)(lambda: copy_table_a().wait_send())
+    pl.when(has_ahead)(lambda: copy_table_b().wait_send())
+    for r in range(steps):
         copy_ya(r).wait_send()
         copy_yb(r).wait_send()
         pl.when(has_behind)(functools.partial(lambda q: copy_xa(q).wait_send(), r))
         pl.when(has_ahead)(functools.partial(lambda q: copy_xb(q).wait_send(), r))
+    for step in range(steps):
+        for k in range(4):
+            copy_corner(step, k).wait_send()
 
 
 def write(v, s, m, out_v, out_s, out_m, sems):
@@ -355,7 +520,8 @@
     steps = src_wave.shape[1]
     grid = lame_lambda.shape[1:]
     nx, ny, nz = grid
-    rounds = 2 * steps
+    rounds = steps
+    corners = 4 * steps
     hbm = pl.BlockSpec(memory_space=pltpu.HBM)
     vmem = pl.BlockSpec(memory_space=pltpu.VMEM)
     big = (velocity, stress, memory, lame_lambda, lame_mu, buoyancy, decay, loss)
@@ -374,19 +540,22 @@
             pltpu.VMEM((n * TZ, 128), F32),
             pltpu.VMEM((n * TZ, 128), F32),
             pltpu.VMEM((steps,) + grid, F32),
-            pltpu.VMEM((rounds, 2, ny, nz), jnp.bfloat16),
-            pltpu.VMEM((rounds, 2, ny, nz), jnp.bfloat16),
-            pltpu.VMEM((rounds, 2, ny, nz), F32),
-            pltpu.VMEM((rounds, 8, nz), F32),
-            pltpu.VMEM((rounds, 8, nz), F32),
-            pltpu.VMEM((rounds, 8, nz), F32),
-            pltpu.VMEM((rounds, 8, nz), F32),
+            pltpu.VMEM((rounds, 6, ny, nz), jnp.bfloat16),
+            pltpu.VMEM((rounds, 6, ny, nz), jnp.bfloat16),
+            pltpu.VMEM((rounds, 6, ny, nz), F32),
+            pltpu.VMEM((rounds, 6, ny, nz), F32),
+        ] + [pltpu.VMEM((rounds, 32, nz), F32)] * 4
+        + [pltpu.VMEM((corners, 8, nz), F32)] * 2 + [
+            pltpu.VMEM((8, nz), F32),
+            pltpu.VMEM((2, 8, nz), F32),
             pltpu.SemaphoreType.DMA((8,)),
             pltpu.SemaphoreType.DMA((len(small),)),
             pltpu.SemaphoreType.DMA,
             pltpu.SemaphoreType.DMA,
-            pltpu.SemaphoreType.DMA((4 * rounds,)),
-            pltpu.SemaphoreType.DMA((4 * rounds,)),
+            pltpu.SemaphoreType.DMA((4 * rounds + 2,)),
+            pltpu.SemaphoreType.DMA((4 * rounds + 2,)),
+            pltpu.SemaphoreType.DMA((corners,)),
+            pltpu.SemaphoreType.DMA((corners,)),
         ],
         compiler_params=pltpu.CompilerParams(
             collective_id=0, has_side_effects=True, vmem_limit_bytes=VMEM_LIMIT

time: 27.7 us -> 23.4 us (0.84)
  Pallas kernels: 26.8 us -> 22.6 us
    pallas_call x1, Pallas kernels: 24.7 us -> 20.4 us  [body(): pl.pallas_call(functools.partial(kernel, n, steps), out_shape=tuple((jax....]
where the time goes in v5:
time: 23.4 us; the launch traced here: 23.2 us
  Pallas kernels  22.6 us (97%)
  between operations  0.64 us (3%)
    pallas_call x1, Pallas kernels, body(): pl.pallas_call(functools.partial(kernel, n, steps), out_shape=tuple((jax....  20.4 us
    pallas_call x1, Pallas kernels, body(): pl.pallas_call(write, out_shape=tuple((jax.ShapeDtypeStruct(a.shape, F32)...  2.17 us

profile of v5, /device:TPU:0, one launch (start us, length us, event | category | flops | bytes accessed | tf_op | source)
XLA Modules:
  0.0 23.2 jit_solution(11183336866191336074)
XLA Ops:
  0.6 20.4 %shard_map.166 = (f32[3,4,32,128]{3,2,1,0:T(8,128)}, f32[6,4,32,128]{3,2,1,0:T(8,128)}, f32[6,4,32,128]{3,2,1,0:T(8,128)}) custom-call(f32[3,1,4,32,128]{4,3,2,1,0:T(8,128)} %vel.1, f32[6,1,4,32,128]{4,3,2,1,0:T(8,128)} %stress.1, f32[6,1,4,32,128]{4,3,2,1,0:T(8,128)} %mem.1, f32[1,4,32,128]{3,2,1,0:T(8,128)} %lam.1, f32[1,4,32,128]{3,2,1,0:T(8,128)} %mu.1, ...), custom_call_target="tpu_custom_call" | custom-call | tf_op jit(solution)/shard_map/pallas_call | solution.py:530
  21.1 2.2 %shard_map.167 = (f32[3,1,4,32,128]{4,3,2,1,0:T(8,128)}, f32[6,1,4,32,128]{4,3,2,1,0:T(8,128)}, f32[6,1,4,32,128]{4,3,2,1,0:T(8,128)}) custom-call(f32[3,4,32,128]{3,2,1,0:T(8,128)} %get-tuple-element.6.v, f32[6,4,32,128]{3,2,1,0:T(8,128)} %get-tuple-element.7.s, f32[6,4,32,128]{3,2,1,0:T(8,128)} %get-tuple-element.8.m), custom_call_target="tpu_custom_call" | custom-call | tf_op jit(solution)/shard_map/pallas_call | solution.py:564
